TPU v7x, 512 devices: a whole 4x8x8 slice. The times are simulated.
512 devices in a mesh: elec: 64 (over x, y, core), therm: 8 (over z).
Axes of the slice: x: 4, y: 8, z: 8, core: 2. Of those that a mesh axis runs over, the one named last changes fastest.
Arguments:
- injected_amperage: bfloat16 [16384, 64, 128], P(('elec', 'therm')), may hold values from -6 to 6
- voltage_self_admittance: float32 [16384, 64], P(('elec', 'therm')), may hold values from 1.2 to 2.5
- voltage_coupling_tiles: bfloat16 [16384, 4, 64, 64], P(('elec', 'therm')), may hold values from -0.5 to 0.5
- voltage_partner_tile_ids: int32 [16384, 4], P(('elec', 'therm')), may hold values from 0 to 31
- interface_tiles_per_level: int32 [2048, 2], P(('elec', 'therm')), may hold values from 0 to 31
- interface_admittance: bfloat16 [4096, 64, 64], P(('elec', 'therm')), may hold values from -0.5 to 0.5
- warmth_receiver_layer: int32 [16384, 1], P(('elec', 'therm')), may hold values from 0 to 7; in each aligned block of 32 rows (0 to 31, 32 to 63, ...) at most 8 rows name the same one
- warmth_receiver_tile: int32 [16384], P(('elec', 'therm')), may hold values from 0 to 31
- warmth_values: bfloat16 [16384, 64, 128], P(('elec', 'therm')), may hold values from -4 to 4
- warmth_self_coefficient: float32 [16384, 64], P(('elec', 'therm')), may hold values from 1 to 3
- warmth_coupling_tiles: bfloat16 [16384, 3, 64, 64], P(('elec', 'therm')), may hold values from -0.4375 to 0.4375
- warmth_partner_tile_ids: int32 [16384, 3], P(('elec', 'therm')), may hold values from 0 to 31
- layer_boundary_couplings: bfloat16 [2048, 64, 64], P(('elec', 'therm')), may hold values from -0.4375 to 0.4375
- substance_kind: int32 [16384, 64], P(('elec', 'therm')), may hold values from 0 to 7
- reference_material_kappas: float32 [8], replicated, may hold values from 0.5 to 4
- warmth_storage_per_point: float32 [16384, 64], P(('elec', 'therm')), may hold values from 1 to 4
Outputs:
- voltage_solution: bfloat16 [16384, 64, 128], P(('elec', 'therm'))
- advanced_warmth_values: float32 [16384, 64, 128], P(('elec', 'therm'))
Inputs may be any that keep to these rules, and one draw needn't show every extreme that they name: `warmth_receiver_layer`: among the 32 blocks of one device at most 8 name the same owner, and exactly 8 do for some owner. `voltage_partner_tile_ids`: indexes a block of the same device. `interface_tiles_per_level`: indexes a block of the same device. `warmth_receiver_tile`: indexes a thermal block of the owner. `warmth_partner_tile_ids`: indexes a thermal block of the same device.
All inputs are finite; a program needn't handle non-finite values.
Results may differ from a plain program's by a relative error of at most 0.025.
Values may be sent and summed in bfloat16 or wider, within the bound.
A program may use at most 64 MiB of HBM per device.

v0:
```python
import jax
import jax.numpy as jnp
from jax import lax
from jax.sharding import PartitionSpec as P

SWEEPS = 5
ZB = 2


relax_factor = 0.8
time_increment = 0.5


def from_partner(block, axis, bit):
    count = lax.axis_size(axis)
    route = []
    for low in range(count):
        high = low | 1 << bit
        if high != low and high < count:
            route += [(low, high), (high, low)]
    return lax.ppermute(block, axis, route)


def with_halo(x, sides, width):
    for axis, dim in sides:
        size, length = (lax.axis_size(axis), x.shape[dim])
        up = [(i, (i + 1) % size) for i in range(size - 1)]
        down = [(j, i) for i, j in up]
        last = lax.slice_in_dim(x, length - width, length, axis=dim)
        first = lax.slice_in_dim(x, 0, width, axis=dim)
        before = lax.ppermute(last, axis, up)
        after = lax.ppermute(first, axis, down)
        x = jnp.concatenate([before, x, after], axis=dim)
    return x


def near_product(field_b, near_blocks, near_index):
    picked = field_b[near_index]
    return jnp.einsum("rkab,rkbc->rac", near_blocks, picked, preferred_element_type=jnp.float32)


def electric_apply(
    field_b,
    voltage_self_admittance,
    voltage_coupling_tiles,
    voltage_partner_tile_ids,
    interface_tiles_per_level,
    interface_admittance,
):
    total = voltage_self_admittance[:, :, None] * field_b.astype(jnp.float32) + near_product(
        field_b, voltage_coupling_tiles, voltage_partner_tile_ids
    )
    received = []
    for level_bit in range(interface_tiles_per_level.shape[0]):
        outgoing = field_b[interface_tiles_per_level[level_bit]]
        received.append(from_partner(outgoing, "elec", level_bit))
    incoming = jnp.concatenate(received, axis=0)
    face_terms = jnp.einsum(
        "sab,sbc->sac", interface_admittance, incoming, preferred_element_type=jnp.float32
    )
    targets = interface_tiles_per_level.reshape(-1)
    selector = (targets[None, :] == jnp.arange(field_b.shape[0])[:, None]).astype(jnp.float32)
    spread = jnp.dot(
        selector, face_terms.reshape(face_terms.shape[0], -1), precision=lax.Precision.HIGHEST
    )
    return total + spread.reshape(total.shape)


def body(
    injected_amperage,
    voltage_self_admittance,
    voltage_coupling_tiles,
    voltage_partner_tile_ids,
    interface_tiles_per_level,
    interface_admittance,
    warmth_receiver_layer,
    warmth_receiver_tile,
    warmth_values,
    warmth_self_coefficient,
    warmth_coupling_tiles,
    warmth_partner_tile_ids,
    layer_boundary_couplings,
    substance_kind,
    reference_material_kappas,
    warmth_storage_per_point,
):
    source = injected_amperage.astype(jnp.float32)
    potential_f = relax_factor * source / voltage_self_admittance[:, :, None]
    for sweep_index in range(SWEEPS - 1):
        field_b = potential_f.astype(jnp.bfloat16)
        image = electric_apply(
            field_b,
            voltage_self_admittance,
            voltage_coupling_tiles,
            voltage_partner_tile_ids,
            interface_tiles_per_level,
            interface_admittance,
        )
        potential_f = (
            potential_f + relax_factor * (source - image) / voltage_self_admittance[:, :, None]
        )
    voltage_solution = potential_f.astype(jnp.bfloat16)
    current = electric_apply(
        voltage_solution,
        voltage_self_admittance,
        voltage_coupling_tiles,
        voltage_partner_tile_ids,
        interface_tiles_per_level,
        interface_admittance,
    )
    heat_b = (voltage_solution.astype(jnp.float32) * current).astype(jnp.bfloat16)
    owners = warmth_receiver_layer[:, 0]
    warmth_tile_count = warmth_values.shape[0]
    block_ids = jnp.arange(warmth_tile_count)[:, None]
    own_index = lax.axis_index("therm")
    heat_piece = lax.all_gather(heat_b, "therm", axis=0, tiled=True)
    owner_piece = lax.all_gather(owners, "therm", axis=0, tiled=True)
    row_piece = lax.all_gather(warmth_receiver_tile, "therm", axis=0, tiled=True)
    selector = ((row_piece[None, :] == block_ids) & (owner_piece[None, :] == own_index)).astype(
        jnp.bfloat16
    )
    resistive_dissipation = jnp.einsum(
        "jr,rbc->jbc", selector, heat_piece, preferred_element_type=jnp.float32
    )
    warmth_distribution = warmth_values.astype(jnp.float32)
    material_hits = (
        substance_kind[:, :, None] == jnp.arange(reference_material_kappas.shape[0])[None, None, :]
    ).astype(jnp.float32)
    pass_along = jnp.sum(material_hits * reference_material_kappas[None, None, :], axis=2)
    diffusivity_coefficient = pass_along[:, :, None] * (1.0 + 0.4 * jnp.tanh(warmth_distribution))
    stream_flow_second = (diffusivity_coefficient * warmth_distribution).astype(jnp.bfloat16)
    padded = with_halo(stream_flow_second, (("therm", 0),), ZB)
    below = padded[:ZB]
    above = padded[padded.shape[0] - ZB :]
    warmth_spread_operator = warmth_self_coefficient[:, :, None] * stream_flow_second.astype(
        jnp.float32
    ) + near_product(stream_flow_second, warmth_coupling_tiles, warmth_partner_tile_ids)
    low_terms = jnp.einsum(
        "zab,zbc->zac", layer_boundary_couplings[:ZB], below, preferred_element_type=jnp.float32
    )
    high_terms = jnp.einsum(
        "zab,zbc->zac", layer_boundary_couplings[ZB:], above, preferred_element_type=jnp.float32
    )
    warmth_spread_operator = (
        warmth_spread_operator.at[:ZB].add(low_terms).at[warmth_tile_count - ZB :].add(high_terms)
    )
    advanced_warmth_values = (
        warmth_distribution
        + time_increment
        * (resistive_dissipation - warmth_spread_operator)
        / warmth_storage_per_point[:, :, None]
    )
    return (voltage_solution, advanced_warmth_values)


def solution(mesh):
    return jax.shard_map(
        body,
        mesh=mesh,
        in_specs=(
            P(("elec", "therm"), None, None),
            P(("elec", "therm"), None),
            P(("elec", "therm"), None, None, None),
            P(("elec", "therm"), None),
            P(("elec", "therm"), None),
            P(("elec", "therm"), None, None),
            P(("elec", "therm"), None),
            P(("elec", "therm")),
            P(("elec", "therm"), None, None),
            P(("elec", "therm"), None),
            P(("elec", "therm"), None, None, None),
            P(("elec", "therm"), None),
            P(("elec", "therm"), None, None),
            P(("elec", "therm"), None),
            P(),
            P(("elec", "therm"), None),
        ),
        out_specs=(P(("elec", "therm"), None, None), P(("elec", "therm"), None, None)),
        check_vma=False,
    )
```

profile of v0, /device:TPU:6, one launch (start us, length us, event | category | flops | bytes accessed | tf_op | source)
XLA Modules:
  0.0 200.5 jit_solution(17127404310122124780)
XLA Ops:
  10.3 7.7 %collective-permute-start.3 = (bf16[2,64,128]{2,1,0:T(8,128)(2,1)S(1)}, bf16[2,64,128]{2,1,0:T(8,128)(2,1)S(1)}, u32[]{:S(2)}, u32[]{:S(2)}) collective-permute-start(bf16[2,64,128]{2,1,0:T(8,128)(2,1)S(1)} %gather_fusion.4), channel_id=1, source_target_pairs={{0,64},{64,0},{8,72},{72,8},{16,80},{80,16},{24,88},{88,24},{32,96... | collective-permute-start | bytes 98312 | tf_op jit(solution)/shard_map/ppermute | solution.py:21
  18.6 2.7 %collective-permute-start.2 = (bf16[2,64,128]{2,1,0:T(8,128)(2,1)S(1)}, bf16[2,64,128]{2,1,0:T(8,128)(2,1)S(1)}, u32[]{:S(2)}, u32[]{:S(2)}) collective-permute-start(bf16[2,64,128]{2,1,0:T(8,128)(2,1)S(1)} %gather_fusion.3), channel_id=1, source_target_pairs={{0,32},{32,0},{8,40},{40,8},{16,48},{48,16},{24,56},{56,24},{64,96... | collective-permute-start | bytes 98312 | tf_op jit(solution)/shard_map/ppermute | solution.py:21
  21.9 2.6 %collective-permute-start.1 = (bf16[2,64,128]{2,1,0:T(8,128)(2,1)S(1)}, bf16[2,64,128]{2,1,0:T(8,128)(2,1)S(1)}, u32[]{:S(2)}, u32[]{:S(2)}) collective-permute-start(bf16[2,64,128]{2,1,0:T(8,128)(2,1)S(1)} %gather_fusion.2), channel_id=1, source_target_pairs={{0,16},{16,0},{8,24},{24,8},{32,48},{48,32},{40,56},{56,40},{64,80... | collective-permute-start | bytes 98312 | tf_op jit(solution)/shard_map/ppermute | solution.py:21
  31.8 4.2 %fusion.120 = (bf16[32,64,128]{2,1,0:T(8,128)(2,1)S(1)}, f32[32,64,128]{2,1,0:T(8,128)}) fusion(f32[32,64,128]{2,0,1:T(8,128)S(1)} %fusion.49, bf16[32,4,64,64]{3,2,1,0:T(8,128)(2,1)S(1)} %copy-done, bf16[32,4,64,128]{3,2,1,0:T(8,128)(2,1)} %bitcast.203, f32[32,64]{1,0:T(8,128)S(1)} %copy-done.3, bf16[32,64,128]{2,1,0:T(8,128)(2,1)} %param.20), kind=kOutput, calls=%fused_computation.184 | convolution fusion | flops 137625600 | bytes 6299648 | tf_op jit(solution)/shard_map/rkab,rkbc->rac/dot_general | solution.py:39
  38.3 4.7 %collective-permute-start.7 = (bf16[2,64,128]{2,1,0:T(8,128)(2,1)S(1)}, bf16[2,64,128]{2,1,0:T(8,128)(2,1)S(1)}, u32[]{:S(2)}, u32[]{:S(2)}) collective-permute-start(bf16[2,64,128]{2,1,0:T(8,128)(2,1)S(1)} %gather_fusion.9), channel_id=1, source_target_pairs={{0,64},{64,0},{8,72},{72,8},{16,80},{80,16},{24,88},{88,24},{32,96... | collective-permute-start | bytes 98312 | tf_op jit(solution)/shard_map/ppermute | solution.py:21
  45.2 2.4 %collective-permute-start.5 = (bf16[2,64,128]{2,1,0:T(8,128)(2,1)S(1)}, bf16[2,64,128]{2,1,0:T(8,128)(2,1)S(1)}, u32[]{:S(2)}, u32[]{:S(2)}) collective-permute-start(bf16[2,64,128]{2,1,0:T(8,128)(2,1)S(1)} %gather_fusion.7), channel_id=1, source_target_pairs={{0,16},{16,0},{8,24},{24,8},{32,48},{48,32},{40,56},{56,40},{64,80... | collective-permute-start | bytes 98312 | tf_op jit(solution)/shard_map/ppermute | solution.py:21
  52.6 4.5 %fusion.121 = (bf16[32,64,128]{2,1,0:T(8,128)(2,1)S(1)}, f32[32,64,128]{2,1,0:T(8,128)}) fusion(f32[32,64,128]{2,1,0:T(8,128)} %get-tuple-element.43, f32[32,64,128]{2,0,1:T(8,128)S(1)} %fusion.47, bf16[32,4,64,64]{3,2,1,0:T(8,128)(2,1)S(1)} %copy-done, bf16[32,4,64,128]{3,2,1,0:T(8,128)(2,1)} %bitcast.201, ...), kind=kOutput, calls=%fused_computation.185 | convolution fusion | flops 136839168 | bytes 7872512 | tf_op jit(solution)/shard_map/rkab,rkbc->rac/dot_general | solution.py:39
  59.4 7.7 %collective-permute-start.11 = (bf16[2,64,128]{2,1,0:T(8,128)(2,1)S(1)}, bf16[2,64,128]{2,1,0:T(8,128)(2,1)S(1)}, u32[]{:S(2)}, u32[]{:S(2)}) collective-permute-start(bf16[2,64,128]{2,1,0:T(8,128)(2,1)S(1)} %gather_fusion.14), channel_id=1, source_target_pairs={{0,64},{64,0},{8,72},{72,8},{16,80},{80,16},{24,88},{88,24},{32,96... | collective-permute-start | bytes 98312 | tf_op jit(solution)/shard_map/ppermute | solution.py:21
  67.1 2.7 %collective-permute-start.10 = (bf16[2,64,128]{2,1,0:T(8,128)(2,1)S(1)}, bf16[2,64,128]{2,1,0:T(8,128)(2,1)S(1)}, u32[]{:S(2)}, u32[]{:S(2)}) collective-permute-start(bf16[2,64,128]{2,1,0:T(8,128)(2,1)S(1)} %gather_fusion.13), channel_id=1, source_target_pairs={{0,32},{32,0},{8,40},{40,8},{16,48},{48,16},{24,56},{56,24},{64,96... | collective-permute-start | bytes 98312 | tf_op jit(solution)/shard_map/ppermute | solution.py:21
  69.8 2.6 %collective-permute-start.9 = (bf16[2,64,128]{2,1,0:T(8,128)(2,1)S(1)}, bf16[2,64,128]{2,1,0:T(8,128)(2,1)S(1)}, u32[]{:S(2)}, u32[]{:S(2)}) collective-permute-start(bf16[2,64,128]{2,1,0:T(8,128)(2,1)S(1)} %gather_fusion.12), channel_id=1, source_target_pairs={{0,16},{16,0},{8,24},{24,8},{32,48},{48,32},{40,56},{56,40},{64,80... | collective-permute-start | bytes 98312 | tf_op jit(solution)/shard_map/ppermute | solution.py:21
  77.4 4.5 %fusion.122 = (bf16[32,64,128]{2,1,0:T(8,128)(2,1)S(1)}, f32[32,64,128]{2,1,0:T(8,128)}) fusion(f32[32,64,128]{2,1,0:T(8,128)} %get-tuple-element.45, f32[32,64,128]{2,0,1:T(8,128)S(1)} %fusion.45, bf16[32,4,64,64]{3,2,1,0:T(8,128)(2,1)S(1)} %copy-done, bf16[32,4,64,128]{3,2,1,0:T(8,128)(2,1)} %bitcast.202, ...), kind=kOutput, calls=%fused_computation.186 | convolution fusion | flops 136839168 | bytes 7872512 | tf_op jit(solution)/shard_map/rkab,rkbc->rac/dot_general | solution.py:39
  84.2 4.7 %collective-permute-start.15 = (bf16[2,64,128]{2,1,0:T(8,128)(2,1)S(1)}, bf16[2,64,128]{2,1,0:T(8,128)(2,1)S(1)}, u32[]{:S(2)}, u32[]{:S(2)}) collective-permute-start(bf16[2,64,128]{2,1,0:T(8,128)(2,1)S(1)} %gather_fusion.19), channel_id=1, source_target_pairs={{0,64},{64,0},{8,72},{72,8},{16,80},{80,16},{24,88},{88,24},{32,96... | collective-permute-start | bytes 98312 | tf_op jit(solution)/shard_map/ppermute | solution.py:21
  91.1 2.4 %collective-permute-start.13 = (bf16[2,64,128]{2,1,0:T(8,128)(2,1)S(1)}, bf16[2,64,128]{2,1,0:T(8,128)(2,1)S(1)}, u32[]{:S(2)}, u32[]{:S(2)}) collective-permute-start(bf16[2,64,128]{2,1,0:T(8,128)(2,1)S(1)} %gather_fusion.17), channel_id=1, source_target_pairs={{0,16},{16,0},{8,24},{24,8},{32,48},{48,32},{40,56},{56,40},{64,80... | collective-permute-start | bytes 98312 | tf_op jit(solution)/shard_map/ppermute | solution.py:21
  98.6 3.5 %fusion.26 = bf16[32,64,128]{2,1,0:T(8,128)(2,1)S(1)} fusion(f32[32,64,128]{2,1,0:T(8,128)} %get-tuple-element.47, bf16[32,4,64,64]{3,2,1,0:T(8,128)(2,1)S(1)} %copy-done, bf16[32,4,64,128]{3,2,1,0:T(8,128)(2,1)} %bitcast.204, bf16[32,64,128]{2,1,0:T(8,128)(2,1)} %param.20, f32[32,64,128]{2,0,1:T(8,128)S(1)} %fusion.43, ...), kind=kOutput, calls=%fused_computation.63 | convolution fusion | flops 136839168 | bytes 6823936 | tf_op jit(solution)/shard_map/rkab,rkbc->rac/dot_general | solution.py:39
  104.5 7.7 %collective-permute-start.19 = (bf16[2,64,128]{2,1,0:T(8,128)(2,1)S(1)}, bf16[2,64,128]{2,1,0:T(8,128)(2,1)S(1)}, u32[]{:S(2)}, u32[]{:S(2)}) collective-permute-start(bf16[2,64,128]{2,1,0:T(8,128)(2,1)S(1)} %gather_fusion.24), channel_id=1, source_target_pairs={{0,64},{64,0},{8,72},{72,8},{16,80},{80,16},{24,88},{88,24},{32,96... | collective-permute-start | bytes 98312 | tf_op jit(solution)/shard_map/ppermute | solution.py:21
  112.2 2.7 %collective-permute-start.18 = (bf16[2,64,128]{2,1,0:T(8,128)(2,1)S(1)}, bf16[2,64,128]{2,1,0:T(8,128)(2,1)S(1)}, u32[]{:S(2)}, u32[]{:S(2)}) collective-permute-start(bf16[2,64,128]{2,1,0:T(8,128)(2,1)S(1)} %gather_fusion.23), channel_id=1, source_target_pairs={{0,32},{32,0},{8,40},{40,8},{16,48},{48,16},{24,56},{56,24},{64,96... | collective-permute-start | bytes 98312 | tf_op jit(solution)/shard_map/ppermute | solution.py:21
  114.9 2.6 %collective-permute-start.17 = (bf16[2,64,128]{2,1,0:T(8,128)(2,1)S(1)}, bf16[2,64,128]{2,1,0:T(8,128)(2,1)S(1)}, u32[]{:S(2)}, u32[]{:S(2)}) collective-permute-start(bf16[2,64,128]{2,1,0:T(8,128)(2,1)S(1)} %gather_fusion.22), channel_id=1, source_target_pairs={{0,16},{16,0},{8,24},{24,8},{32,48},{48,32},{40,56},{56,40},{64,80... | collective-permute-start | bytes 98312 | tf_op jit(solution)/shard_map/ppermute | solution.py:21
  122.5 3.9 %fusion.23 = bf16[32,64,128]{2,1,0:T(8,128)(2,1)} fusion(bf16[32,4,64,64]{3,2,1,0:T(8,128)(2,1)S(1)} %copy-done, bf16[32,4,64,128]{3,2,1,0:T(8,128)(2,1)} %bitcast.199, bf16[32,64,128]{2,1,0:T(8,128)(2,1)S(1)} %fusion.26, f32[32,64,128]{2,0,1:T(8,128)S(1)} %fusion.41, f32[32,64]{1,0:T(8,128)S(1)} %copy-done.3), kind=kOutput, calls=%fused_computation.60 | convolution fusion | flops 135790592 | bytes 5251072 | tf_op jit(solution)/shard_map/rkab,rkbc->rac/dot_general | solution.py:39
  127.2 4.3 %collective-permute-start.20 = (bf16[2,64,128]{2,0,1:T(2,128)(2,1)S(1)}, bf16[2,64,128]{2,0,1:T(2,128)(2,1)S(1)}, u32[]{:S(2)}, u32[]{:S(2)}) collective-permute-start(bf16[2,64,128]{2,0,1:T(2,128)(2,1)S(1)} %get-tuple-element.41), channel_id=1, source_target_pairs={{0,1},{1,2},{2,3},{3,4},{4,5},{5,6},{6,7},{8,9},{9,10},{10,11},{11... | collective-permute-start | bytes 98312 | tf_op jit(solution)/shard_map/ppermute | solution.py:31
  137.6 19.4 %all-reduce.2 = (s32[256]{0:T(256)S(1)}, s32[256]{0:T(256)S(1)}) all-reduce(s32[256]{0:T(256)S(1)} %dynamic-update-slice.6, s32[256]{0:T(256)S(1)} %bitcast_dynamic-update-slice_fusion), channel_id=1, replica_groups=mesh['elec'=64,'therm'=8] {'therm'}, use_global_device_ids=true, to_apply=%add | all-reduce | flops 512 | bytes 4096
  157.0 2.6 %convolution_bitcast_fusion = f32[32,128,64]{1,2,0:T(8,128)S(1)} fusion(bf16[32,3,64,64]{3,2,1,0:T(8,128)(2,1)} %param.30, bf16[32,3,64,128]{3,2,1,0:T(8,128)(2,1)} %bitcast.200), kind=kOutput, calls=%fused_computation.37 | convolution fusion | flops 100663296 | bytes 3407872 | tf_op jit(solution)/shard_map/rkab,rkbc->rac/dot_general | solution.py:39
  159.7 3.1 %bitcast_add_fusion = f32[32,64,128]{2,0,1:T(8,128)} fusion(f32[32,128,64]{1,2,0:T(8,128)S(1)} %convolution_bitcast_fusion, f32[32,64]{0,1:T(8,128)S(1)} %copy.82, bf16[32,64,128]{2,1,0:T(8,128)(2,1)S(1)} %copy-done.2, f32[32,64]{0,1:T(8,128)S(1)} %copy.83), kind=kLoop, calls=%fused_computation.80 | loop fusion | flops 2359296 | bytes 2637824 | tf_op jit(solution)/shard_map/add | solution.py:135
  166.5 20.3 %all-gather.3.cloned.1.call-done = bf16[256,64,128]{2,1,0:T(8,128)(2,1)} async-done(((bf16[32,64,128]{2,1,0:T(8,128)(2,1)}), bf16[256,64,128]{2,1,0:T(8,128)(2,1)}) %all-gather.3.cloned.1.call-update) | async-done | bytes 4194320 | tf_op jit(solution)/shard_map/all_gather | solution.py:116
  186.9 5.2 %convert_add_fusion = f32[32,64,128]{2,0,1:T(8,128)S(1)} fusion(f32[32,64,128]{2,0,1:T(8,128)} %fusion.86, bf16[256,64,128]{2,1,0:T(8,128)(2,1)} %all-gather.3.cloned.1.call-done, f32[32,64]{0,1:T(8,128)S(1)} %copy.91, bf16[32,64,128]{2,1,0:T(8,128)(2,1)S(1)} %copy-done.2, s32[256]{0:T(256)S(1)} %get-tuple-element.38, ...), kind=kOutput, calls=%fused_computation.33 | convolution fusion | flops 135544832 | bytes 6825216 | tf_op jit(solution)/shard_map/jr,rbc->jbc/dot_general | solution.py:122
  (130 shorter events, 56.2 us)
Async XLA Ops:
  7.2 24.6 %copy-start = (bf16[32,4,64,64]{3,2,1,0:T(8,128)(2,1)S(1)}, bf16[32,4,64,64]{3,2,1,0:T(8,128)(2,1)}, u32[]{:S(2)}) copy-start(bf16[32,4,64,64]{3,2,1,0:T(8,128)(2,1)} %param.22) | copy-start | bytes 3145732
  7.2 179.7 %all-gather.3.cloned.1.call-start = ((), (), s32[]{:S(2)}) async-start(), calls=%async_computation | async-start | bytes 4718592 | tf_op jit(solution)/shard_map/all_gather | solution.py:116
  10.3 20.6 %collective-permute-start.3 = (bf16[2,64,128]{2,1,0:T(8,128)(2,1)S(1)}, bf16[2,64,128]{2,1,0:T(8,128)(2,1)S(1)}, u32[]{:S(2)}, u32[]{:S(2)}) collective-permute-start(bf16[2,64,128]{2,1,0:T(8,128)(2,1)S(1)} %gather_fusion.4), channel_id=1, source_target_pairs={{0,64},{64,0},{8,72},{72,8},{16,80},{80,16},{24,88},{88,24},{32,96... | collective-permute-start | bytes 98312 | tf_op jit(solution)/shard_map/ppermute | solution.py:21
  18.6 12.3 %collective-permute-start.2 = (bf16[2,64,128]{2,1,0:T(8,128)(2,1)S(1)}, bf16[2,64,128]{2,1,0:T(8,128)(2,1)S(1)}, u32[]{:S(2)}, u32[]{:S(2)}) collective-permute-start(bf16[2,64,128]{2,1,0:T(8,128)(2,1)S(1)} %gather_fusion.3), channel_id=1, source_target_pairs={{0,32},{32,0},{8,40},{40,8},{16,48},{48,16},{24,56},{56,24},{64,96... | collective-permute-start | bytes 98312 | tf_op jit(solution)/shard_map/ppermute | solution.py:21
  21.9 9.0 %collective-permute-start.1 = (bf16[2,64,128]{2,1,0:T(8,128)(2,1)S(1)}, bf16[2,64,128]{2,1,0:T(8,128)(2,1)S(1)}, u32[]{:S(2)}, u32[]{:S(2)}) collective-permute-start(bf16[2,64,128]{2,1,0:T(8,128)(2,1)S(1)} %gather_fusion.2), channel_id=1, source_target_pairs={{0,16},{16,0},{8,24},{24,8},{32,48},{48,32},{40,56},{56,40},{64,80... | collective-permute-start | bytes 98312 | tf_op jit(solution)/shard_map/ppermute | solution.py:21
  25.1 5.9 %collective-permute-start = (bf16[2,64,128]{2,1,0:T(8,128)(2,1)S(1)}, bf16[2,64,128]{2,1,0:T(8,128)(2,1)S(1)}, u32[]{:S(2)}, u32[]{:S(2)}) collective-permute-start(bf16[2,64,128]{2,1,0:T(8,128)(2,1)S(1)} %gather_fusion.1), channel_id=1, source_target_pairs={{0,8},{8,0},{16,24},{24,16},{32,40},{40,32},{48,56},{56,48},{64,72... | collective-permute-start | bytes 98312 | tf_op jit(solution)/shard_map/ppermute | solution.py:21
  38.3 13.4 %collective-permute-start.7 = (bf16[2,64,128]{2,1,0:T(8,128)(2,1)S(1)}, bf16[2,64,128]{2,1,0:T(8,128)(2,1)S(1)}, u32[]{:S(2)}, u32[]{:S(2)}) collective-permute-start(bf16[2,64,128]{2,1,0:T(8,128)(2,1)S(1)} %gather_fusion.9), channel_id=1, source_target_pairs={{0,64},{64,0},{8,72},{72,8},{16,80},{80,16},{24,88},{88,24},{32,96... | collective-permute-start | bytes 98312 | tf_op jit(solution)/shard_map/ppermute | solution.py:21
  43.0 8.7 %collective-permute-start.6 = (bf16[2,64,128]{2,1,0:T(8,128)(2,1)S(1)}, bf16[2,64,128]{2,1,0:T(8,128)(2,1)S(1)}, u32[]{:S(2)}, u32[]{:S(2)}) collective-permute-start(bf16[2,64,128]{2,1,0:T(8,128)(2,1)S(1)} %gather_fusion.8), channel_id=1, source_target_pairs={{0,32},{32,0},{8,40},{40,8},{16,48},{48,16},{24,56},{56,24},{64,96... | collective-permute-start | bytes 98312 | tf_op jit(solution)/shard_map/ppermute | solution.py:21
  45.2 6.5 %collective-permute-start.5 = (bf16[2,64,128]{2,1,0:T(8,128)(2,1)S(1)}, bf16[2,64,128]{2,1,0:T(8,128)(2,1)S(1)}, u32[]{:S(2)}, u32[]{:S(2)}) collective-permute-start(bf16[2,64,128]{2,1,0:T(8,128)(2,1)S(1)} %gather_fusion.7), channel_id=1, source_target_pairs={{0,16},{16,0},{8,24},{24,8},{32,48},{48,32},{40,56},{56,40},{64,80... | collective-permute-start | bytes 98312 | tf_op jit(solution)/shard_map/ppermute | solution.py:21
  47.6 4.1 %collective-permute-start.4 = (bf16[2,64,128]{2,1,0:T(8,128)(2,1)S(1)}, bf16[2,64,128]{2,1,0:T(8,128)(2,1)S(1)}, u32[]{:S(2)}, u32[]{:S(2)}) collective-permute-start(bf16[2,64,128]{2,1,0:T(8,128)(2,1)S(1)} %gather_fusion.6), channel_id=1, source_target_pairs={{0,8},{8,0},{16,24},{24,16},{32,40},{40,32},{48,56},{56,48},{64,72... | collective-permute-start | bytes 98312 | tf_op jit(solution)/shard_map/ppermute | solution.py:21
  59.4 17.1 %collective-permute-start.11 = (bf16[2,64,128]{2,1,0:T(8,128)(2,1)S(1)}, bf16[2,64,128]{2,1,0:T(8,128)(2,1)S(1)}, u32[]{:S(2)}, u32[]{:S(2)}) collective-permute-start(bf16[2,64,128]{2,1,0:T(8,128)(2,1)S(1)} %gather_fusion.14), channel_id=1, source_target_pairs={{0,64},{64,0},{8,72},{72,8},{16,80},{80,16},{24,88},{88,24},{32,96... | collective-permute-start | bytes 98312 | tf_op jit(solution)/shard_map/ppermute | solution.py:21
  67.1 9.4 %collective-permute-start.10 = (bf16[2,64,128]{2,1,0:T(8,128)(2,1)S(1)}, bf16[2,64,128]{2,1,0:T(8,128)(2,1)S(1)}, u32[]{:S(2)}, u32[]{:S(2)}) collective-permute-start(bf16[2,64,128]{2,1,0:T(8,128)(2,1)S(1)} %gather_fusion.13), channel_id=1, source_target_pairs={{0,32},{32,0},{8,40},{40,8},{16,48},{48,16},{24,56},{56,24},{64,96... | collective-permute-start | bytes 98312 | tf_op jit(solution)/shard_map/ppermute | solution.py:21
  69.8 6.7 %collective-permute-start.9 = (bf16[2,64,128]{2,1,0:T(8,128)(2,1)S(1)}, bf16[2,64,128]{2,1,0:T(8,128)(2,1)S(1)}, u32[]{:S(2)}, u32[]{:S(2)}) collective-permute-start(bf16[2,64,128]{2,1,0:T(8,128)(2,1)S(1)} %gather_fusion.12), channel_id=1, source_target_pairs={{0,16},{16,0},{8,24},{24,8},{32,48},{48,32},{40,56},{56,40},{64,80... | collective-permute-start | bytes 98312 | tf_op jit(solution)/shard_map/ppermute | solution.py:21
  72.4 4.1 %collective-permute-start.8 = (bf16[2,64,128]{2,1,0:T(8,128)(2,1)S(1)}, bf16[2,64,128]{2,1,0:T(8,128)(2,1)S(1)}, u32[]{:S(2)}, u32[]{:S(2)}) collective-permute-start(bf16[2,64,128]{2,1,0:T(8,128)(2,1)S(1)} %gather_fusion.11), channel_id=1, source_target_pairs={{0,8},{8,0},{16,24},{24,16},{32,40},{40,32},{48,56},{56,48},{64,72... | collective-permute-start | bytes 98312 | tf_op jit(solution)/shard_map/ppermute | solution.py:21
  84.2 13.6 %collective-permute-start.15 = (bf16[2,64,128]{2,1,0:T(8,128)(2,1)S(1)}, bf16[2,64,128]{2,1,0:T(8,128)(2,1)S(1)}, u32[]{:S(2)}, u32[]{:S(2)}) collective-permute-start(bf16[2,64,128]{2,1,0:T(8,128)(2,1)S(1)} %gather_fusion.19), channel_id=1, source_target_pairs={{0,64},{64,0},{8,72},{72,8},{16,80},{80,16},{24,88},{88,24},{32,96... | collective-permute-start | bytes 98312 | tf_op jit(solution)/shard_map/ppermute | solution.py:21
  88.9 8.9 %collective-permute-start.14 = (bf16[2,64,128]{2,1,0:T(8,128)(2,1)S(1)}, bf16[2,64,128]{2,1,0:T(8,128)(2,1)S(1)}, u32[]{:S(2)}, u32[]{:S(2)}) collective-permute-start(bf16[2,64,128]{2,1,0:T(8,128)(2,1)S(1)} %gather_fusion.18), channel_id=1, source_target_pairs={{0,32},{32,0},{8,40},{40,8},{16,48},{48,16},{24,56},{56,24},{64,96... | collective-permute-start | bytes 98312 | tf_op jit(solution)/shard_map/ppermute | solution.py:21
  91.1 6.6 %collective-permute-start.13 = (bf16[2,64,128]{2,1,0:T(8,128)(2,1)S(1)}, bf16[2,64,128]{2,1,0:T(8,128)(2,1)S(1)}, u32[]{:S(2)}, u32[]{:S(2)}) collective-permute-start(bf16[2,64,128]{2,1,0:T(8,128)(2,1)S(1)} %gather_fusion.17), channel_id=1, source_target_pairs={{0,16},{16,0},{8,24},{24,8},{32,48},{48,32},{40,56},{56,40},{64,80... | collective-permute-start | bytes 98312 | tf_op jit(solution)/shard_map/ppermute | solution.py:21
  93.5 4.3 %collective-permute-start.12 = (bf16[2,64,128]{2,1,0:T(8,128)(2,1)S(1)}, bf16[2,64,128]{2,1,0:T(8,128)(2,1)S(1)}, u32[]{:S(2)}, u32[]{:S(2)}) collective-permute-start(bf16[2,64,128]{2,1,0:T(8,128)(2,1)S(1)} %gather_fusion.16), channel_id=1, source_target_pairs={{0,8},{8,0},{16,24},{24,16},{32,40},{40,32},{48,56},{56,48},{64,72... | collective-permute-start | bytes 98312 | tf_op jit(solution)/shard_map/ppermute | solution.py:21
  104.5 17.1 %collective-permute-start.19 = (bf16[2,64,128]{2,1,0:T(8,128)(2,1)S(1)}, bf16[2,64,128]{2,1,0:T(8,128)(2,1)S(1)}, u32[]{:S(2)}, u32[]{:S(2)}) collective-permute-start(bf16[2,64,128]{2,1,0:T(8,128)(2,1)S(1)} %gather_fusion.24), channel_id=1, source_target_pairs={{0,64},{64,0},{8,72},{72,8},{16,80},{80,16},{24,88},{88,24},{32,96... | collective-permute-start | bytes 98312 | tf_op jit(solution)/shard_map/ppermute | solution.py:21
  112.2 9.4 %collective-permute-start.18 = (bf16[2,64,128]{2,1,0:T(8,128)(2,1)S(1)}, bf16[2,64,128]{2,1,0:T(8,128)(2,1)S(1)}, u32[]{:S(2)}, u32[]{:S(2)}) collective-permute-start(bf16[2,64,128]{2,1,0:T(8,128)(2,1)S(1)} %gather_fusion.23), channel_id=1, source_target_pairs={{0,32},{32,0},{8,40},{40,8},{16,48},{48,16},{24,56},{56,24},{64,96... | collective-permute-start | bytes 98312 | tf_op jit(solution)/shard_map/ppermute | solution.py:21
  114.9 6.7 %collective-permute-start.17 = (bf16[2,64,128]{2,1,0:T(8,128)(2,1)S(1)}, bf16[2,64,128]{2,1,0:T(8,128)(2,1)S(1)}, u32[]{:S(2)}, u32[]{:S(2)}) collective-permute-start(bf16[2,64,128]{2,1,0:T(8,128)(2,1)S(1)} %gather_fusion.22), channel_id=1, source_target_pairs={{0,16},{16,0},{8,24},{24,8},{32,48},{48,32},{40,56},{56,40},{64,80... | collective-permute-start | bytes 98312 | tf_op jit(solution)/shard_map/ppermute | solution.py:21
  117.5 4.1 %collective-permute-start.16 = (bf16[2,64,128]{2,1,0:T(8,128)(2,1)S(1)}, bf16[2,64,128]{2,1,0:T(8,128)(2,1)S(1)}, u32[]{:S(2)}, u32[]{:S(2)}) collective-permute-start(bf16[2,64,128]{2,1,0:T(8,128)(2,1)S(1)} %gather_fusion.21), channel_id=1, source_target_pairs={{0,8},{8,0},{16,24},{24,16},{32,40},{40,32},{48,56},{56,48},{64,72... | collective-permute-start | bytes 98312 | tf_op jit(solution)/shard_map/ppermute | solution.py:21
  127.2 35.7 %collective-permute-start.20 = (bf16[2,64,128]{2,0,1:T(2,128)(2,1)S(1)}, bf16[2,64,128]{2,0,1:T(2,128)(2,1)S(1)}, u32[]{:S(2)}, u32[]{:S(2)}) collective-permute-start(bf16[2,64,128]{2,0,1:T(2,128)(2,1)S(1)} %get-tuple-element.41), channel_id=1, source_target_pairs={{0,1},{1,2},{2,3},{3,4},{4,5},{5,6},{6,7},{8,9},{9,10},{10,11},{11... | collective-permute-start | bytes 98312 | tf_op jit(solution)/shard_map/ppermute | solution.py:31
  131.5 31.5 %collective-permute-start.21 = (bf16[2,64,128]{2,0,1:T(2,128)(2,1)S(1)}, bf16[2,64,128]{2,0,1:T(2,128)(2,1)S(1)}, u32[]{:S(2)}, u32[]{:S(2)}) collective-permute-start(bf16[2,64,128]{2,0,1:T(2,128)(2,1)S(1)} %get-tuple-element.40), channel_id=1, source_target_pairs={{1,0},{2,1},{3,2},{4,3},{5,4},{6,5},{7,6},{9,8},{10,9},{11,10},{12... | collective-permute-start | bytes 98312 | tf_op jit(solution)/shard_map/ppermute | solution.py:32
  (12 other events, 69.3 us)
Sparse Core Ops, SparseCore 0:
  126.6 60.2 all-gather.2
where the time goes:
time: 202 us; the launch traced here: 200 us
  starting transfers between devices  73.1 us (36%)
  matrix products  33 us (16%)
  local copies, waits for them, and re-layouts  30 us (15%)
  waiting for transfers between devices  20.4 us (10%)
  blocking collectives  19.4 us (10%)
  between operations  15.3 us (8%)
  other arithmetic  9.18 us (5%)
    ppermute x20, starting transfers between devices, from_partner(): return lax.ppermute(block, axis, route)  67.5 us
    dot_general x6, matrix products, near_product(): jnp.einsum('rkab,rkbc->rac', near_blocks, picked, preferred_element_type=...  23.4 us
    all_gather x1, waiting for transfers between devices, body(): heat_piece = lax.all_gather(heat_b, 'therm', axis=0, tiled=True)  20.3 us
    unnamed x1, blocking collectives  19.4 us
    gather x6, local copies, waits for them, and re-layouts, near_product(): picked = field_b[near_index]  12.8 us
    gather x20, local copies, waits for them, and re-layouts, electric_apply(): outgoing = field_b[interface_tiles_per_level[level_bit]]  11.2 us
    dot_general x1, matrix products, body(): jnp.einsum('jr,rbc->jbc', selector, heat_piece, preferred_element_type=jn...  5.19 us
    ppermute x1, starting transfers between devices, with_halo(): before = lax.ppermute(last, axis, up)  4.27 us
  transfers between devices with their start and end apart: 23, of which 1 were waited for; matrix products, arithmetic and copies ran while one was open for 14% of the time, Pallas kernels for 0%

commit v1 on v0

v1 whole, which is shorter than its diff:
```python
import functools

import jax
import jax.numpy as jnp
from jax import lax
from jax.experimental import pallas as pl
from jax.experimental.pallas import tpu as pltpu
from jax.sharding import PartitionSpec as P

MESH = pl.DeviceIdType.MESH
F32 = jnp.float32
BF16 = jnp.bfloat16

SWEEPS = 5
RELAX = 0.8
STEP = 0.5
B = 32
N = 64
C = 128
LEVELS = 4
SLOTS = 8
CAP = 8
NZ = 8
K_E = 4
K_T = 3
ALL = B + SLOTS

AT_IDS = 0
AT_SRC = AT_IDS + B * K_E
AT_OUT = AT_SRC + ALL
AT_PACK = AT_OUT + B
AT_TIDS = AT_PACK + NZ * CAP
AT_END = AT_TIDS + B * K_T


def loop(n, step, unroll=1, start=0):
    def one(i, _):
        step(i)
        return 0

    lax.fori_loop(start, n, one, 0, unroll=unroll)


def kernel(
    tab,
    kappas,
    ends,
    diag_e,
    faces,
    diag_t,
    kind,
    storage,
    rims,
    source_h,
    tiles_h,
    warm_h,
    ttiles_h,
    v_out,
    w_out,
    source,
    tiles,
    warm,
    ttiles,
    turn,
    scale,
    diag,
    start0,
    pot,
    field,
    near,
    wide,
    tnear,
    inc,
    coef,
    acc,
    flux,
    halo,
    heat,
    outgo,
    income,
    prefix,
    vbuf,
    ends_in,
    ends_s,
    local_sem,
    ex_send,
    ex_recv,
    halo_send,
    halo_recv,
    ends_send,
    ends_recv,
    heat_send,
    heat_recv,
):
    e = lax.axis_index("elec")
    t = lax.axis_index("therm")

    def copy_in(src, dst, i):
        return pltpu.make_async_copy(src, dst, local_sem.at[i])

    c_source = copy_in(source_h, source, 0)
    c_tiles = copy_in(tiles_h, tiles, 1)
    c_warm = copy_in(warm_h, warm, 2)
    c_ttiles = copy_in(ttiles_h, ttiles, 3)
    for c in (c_source, c_tiles, c_warm, c_ttiles):
        c.start()

    def partner(bit):
        return e + (1 << bit) - 2 * (1 << bit) * (lax.rem(lax.div(e, 1 << bit), 2))

    barrier = pltpu.get_barrier_semaphore()
    for bit in range(LEVELS):
        pl.semaphore_signal(barrier, inc=1, device_id={"elec": partner(bit)}, device_id_type=MESH)
    for o in range(1, NZ):
        pl.semaphore_signal(
            barrier, inc=1, device_id={"therm": lax.rem(t + o, NZ)}, device_id_type=MESH
        )

    def exchange(k, b):
        return pltpu.make_async_remote_copy(
            src_ref=field.at[k, pl.ds(B + 2 * b, 2)],
            dst_ref=inc.at[k, pl.ds(2 * b, 2)],
            send_sem=ex_send.at[k, b],
            recv_sem=ex_recv.at[k, b],
            device_id={"elec": partner(b)},
            device_id_type=MESH,
        )

    def give(src, dst, send, recv, o):
        return pltpu.make_async_remote_copy(
            src_ref=src,
            dst_ref=dst,
            send_sem=send,
            recv_sem=recv,
            device_id={"therm": lax.rem(t + o, NZ)},
            device_id_type=MESH,
        )

    turn[...] = jnp.zeros_like(turn)
    turn[0:B, 0:N] = RELAX / diag_e[...]
    turn[B : 2 * B, 0:N] = diag_e[...]
    c_source.wait()
    flipped = turn[...].T[0:N, :]

    def first(i, cur):
        s = jnp.broadcast_to(cur[:, 0:1], (N, C))
        d = jnp.broadcast_to(cur[:, B : B + 1], (N, C))
        scale[i] = s
        diag[i] = d
        v = s * source[i].astype(F32)
        start0[i] = v
        pot[i] = v
        field[0, i] = v.astype(BF16)
        return pltpu.roll(cur, C - 1, 1)

    lax.fori_loop(0, B, first, flipped, unroll=2)

    def slot_copy(m):
        i = tab[AT_SRC + m]
        field[0, m] = field[0, i]

    loop(ALL, slot_copy, 8, B)
    pl.semaphore_wait(barrier, LEVELS + NZ - 1)
    for b in reversed(range(LEVELS)):
        exchange(0, b).start()

    c_ends = [give(ends.at[lax.rem(t + o, NZ)], ends_in.at[o], ends_send.at[o], ends_recv.at[o], o) for o in range(1, NZ)]
    for c in c_ends:
        c.start()
    ends_in[0] = ends[t]

    def slot_more(m):
        i = tab[AT_SRC + m]
        scale[m] = scale[i]
        diag[m] = diag[i]
        start0[m] = start0[i]
        pot[m] = start0[i]

    loop(ALL, slot_more, 2, B)

    for s in range(SLOTS):
        for q in range(SLOTS):
            same = (tab[AT_SRC + B + s] == tab[AT_SRC + B + q]).astype(F32)
            wide[s, :, q * N : (q + 1) * N] = (faces[q].astype(F32) * same).astype(BF16)

    c_tiles.wait()

    def lay_e(i):
        near[i] = jnp.concatenate([tiles[i, k] for k in range(K_E)], axis=1)

    loop(B, lay_e, 2)

    def product(k, m):
        i = tab[AT_SRC + m]
        rhs = jnp.concatenate(
            [field[k, tab[AT_IDS + i * K_E + q]] for q in range(K_E)], axis=0
        )
        return jnp.dot(near[i], rhs, preferred_element_type=F32)

    def sweep(k):
        def update(m):
            new = pot[m] + start0[m] - RELAX * field[k, m].astype(F32) - scale[m] * product(k, m)
            pot[m] = new
            return new

        loop(ALL, update, 4, B)

        def natural(m):
            field[k + 1, m] = update(m).astype(BF16)

        loop(B, natural, 4)

    def face_terms(k, then):
        for b in range(LEVELS):
            exchange(k, b).wait_recv()
        rhs = inc[k].reshape(SLOTS * N, C)

        def one(s):
            then(s, jnp.dot(wide[s], rhs, preferred_element_type=F32))

        loop(SLOTS, one, 4)

    def finish(k):
        def then(s, g):
            new = pot[B + s] - scale[B + s] * g
            pot[B + s] = new
            field[k + 1, B + s] = new.astype(BF16)

        face_terms(k, then)
        for b in reversed(range(LEVELS)):
            exchange(k + 1, b).start()

    sweep(0)
    finish(0)

    c_up = give(flux.at[pl.ds(B - 2, 2)], halo.at[pl.ds(0, 2)], halo_send.at[0], halo_recv.at[0], 1)
    c_down = give(flux.at[pl.ds(0, 2)], halo.at[pl.ds(2, 2)], halo_send.at[1], halo_recv.at[1], NZ - 1)
    sweep(1)
    c_warm.wait()
    kap = jnp.zeros((B, N), F32)
    for m in range(8):
        kap = kap + jnp.where(kind[...] == m, kappas[m], 0.0)
    turn[0:B, 0:N] = diag_t[...]
    turn[B : 2 * B, 0:N] = kap
    turn[2 * B : 3 * B, 0:N] = STEP / storage[...]
    tflipped = turn[...].T[0:N, :]

    def warmth(i, cur):
        dt = jnp.broadcast_to(cur[:, 0:1], (N, C))
        ka = jnp.broadcast_to(cur[:, B : B + 1], (N, C))
        co = jnp.broadcast_to(cur[:, 2 * B : 2 * B + 1], (N, C))
        w = warm[i].astype(F32)
        fl = (ka * (1.0 + 0.4 * jnp.tanh(w)) * w).astype(BF16)
        flux[i] = fl
        coef[i] = co
        acc[i] = w - co * (dt * fl.astype(F32))
        return pltpu.roll(cur, C - 1, 1)

    lax.fori_loop(0, B, warmth, tflipped, unroll=2)
    c_up.start()
    c_down.start()
    finish(1)
    sweep(2)
    c_ttiles.wait()

    def lay_t(i):
        tnear[i] = jnp.concatenate([ttiles[i, k] for k in range(K_T)], axis=1)

    loop(B, lay_t, 2)
    finish(2)
    sweep(3)

    def conduct(i):
        rhs = jnp.concatenate([flux[tab[AT_TIDS + i * K_T + q]] for q in range(K_T)], axis=0)
        acc[i] = acc[i] - coef[i] * jnp.dot(tnear[i], rhs, preferred_element_type=F32)

    loop(B, conduct, 4)
    finish(3)

    last = SWEEPS - 1

    def slot_current(m):
        pot[m] = diag[m] * field[last, m].astype(F32) + product(last, m)

    loop(ALL, slot_current, 4, B)

    def natural_heat(m):
        f = field[last, m].astype(F32)
        heat[m] = (f * (diag[m] * f + product(last, m))).astype(BF16)

    loop(B, natural_heat, 4)

    def place(i):
        vbuf[i] = field[last, tab[AT_OUT + i]]

    loop(B, place, 4)
    c_v = copy_in(vbuf, v_out, 4)
    c_v.start()

    c_up.wait()
    c_down.wait()
    for z in range(2):
        low = jnp.dot(rims[z], halo[z], preferred_element_type=F32)
        acc[z] = acc[z] - jnp.where(t > 0, 1.0, 0.0) * coef[z] * low
        high = jnp.dot(rims[2 + z], halo[2 + z], preferred_element_type=F32)
        acc[B - 2 + z] = acc[B - 2 + z] - jnp.where(t < NZ - 1, 1.0, 0.0) * coef[B - 2 + z] * high
    for c in c_ends:
        c.wait()
    c_table = pltpu.make_async_copy(ends_in, ends_s, local_sem.at[5])
    c_table.start()
    c_table.wait()

    def slot_heat(s, g):
        heat[B + s] = (field[last, B + s].astype(F32) * (pot[B + s] + g)).astype(BF16)

    face_terms(last, slot_heat)

    order = (4, 3, 5, 2, 6, 1, 7)
    c_heat = {
        o: give(outgo.at[o], income.at[o], heat_send.at[o], heat_recv.at[o], o) for o in order
    }
    for o in order:
        to = lax.rem(t + o, NZ)
        for s in range(CAP):
            outgo[o, s] = heat[tab[AT_PACK + to * CAP + s]]
        c_heat[o].start()
    for s in range(CAP):
        income[0, s] = heat[tab[AT_PACK + t * CAP + s]]

    def collect(o):
        run = jnp.zeros((N, C), F32)
        prefix[0] = run
        for s in range(CAP):
            run = run + income[o, s].astype(F32)
            prefix[s + 1] = run

        def row(j):
            upto = prefix[ends_s[o, 0, j + 1]]
            before = prefix[ends_s[o, 0, j]]
            acc[j] = acc[j] + coef[j] * (upto - before)

        loop(B, row, 2)

    collect(0)
    for o in order:
        c_heat[o].wait_recv()
        collect(o)
    c_w = copy_in(acc, w_out, 6)
    c_w.start()
    for o in order:
        c_heat[o].wait_send()
    for k in range(SWEEPS):
        for b in range(LEVELS):
            exchange(k, b).wait_send()
    c_v.wait()
    c_w.wait()


def tables(conn, sends, owner, row, tconn):
    targets = sends.reshape(-1)
    far = jnp.int32(1000)
    slot = jnp.arange(SLOTS, dtype=jnp.int32)
    block = jnp.arange(B, dtype=jnp.int32)

    def moved(x):
        hit = jnp.min(jnp.where(x[..., None] == targets, B + slot, far), axis=-1)
        return jnp.where(hit < far, hit, x)

    own = owner[:, 0]
    earlier = (row[None, :] < row[:, None]) | (
        (row[None, :] == row[:, None]) & (block[None, :] < block[:, None])
    )
    rank = jnp.sum(((own[None, :] == own[:, None]) & earlier).astype(jnp.int32), axis=1)
    places = own * CAP + rank
    spots = jnp.arange(NZ * CAP, dtype=jnp.int32)
    at = moved(block)
    pack = jnp.sum(jnp.where(places[None, :] == spots[:, None], at[None, :], 0), axis=1)
    tab = jnp.concatenate(
        [moved(conn).reshape(-1), block, targets, at, pack, tconn.reshape(-1)]
    )
    upto = jnp.arange(C, dtype=jnp.int32)
    z = jnp.arange(NZ, dtype=jnp.int32)
    ends = jnp.sum(
        (
            (own[None, None, :] == z[:, None, None]) & (row[None, None, :] < upto[None, :, None])
        ).astype(jnp.int32),
        axis=2,
    )
    return tab, jnp.broadcast_to(ends[:, None, :], (NZ, 8, C))


def body(
    injected_amperage,
    voltage_self_admittance,
    voltage_coupling_tiles,
    voltage_partner_tile_ids,
    interface_tiles_per_level,
    interface_admittance,
    warmth_receiver_layer,
    warmth_receiver_tile,
    warmth_values,
    warmth_self_coefficient,
    warmth_coupling_tiles,
    warmth_partner_tile_ids,
    layer_boundary_couplings,
    substance_kind,
    reference_material_kappas,
    warmth_storage_per_point,
):
    tab, ends = tables(
        voltage_partner_tile_ids,
        interface_tiles_per_level,
        warmth_receiver_layer,
        warmth_receiver_tile,
        warmth_partner_tile_ids,
    )
    smem = pl.BlockSpec(memory_space=pltpu.SMEM)
    vmem = pl.BlockSpec(memory_space=pltpu.VMEM)
    hbm = pl.BlockSpec(memory_space=pl.ANY)
    dma = pltpu.SemaphoreType.DMA
    V = pltpu.VMEM
    return pl.pallas_call(
        kernel,
        out_shape=(
            jax.ShapeDtypeStruct((B, N, C), BF16),
            jax.ShapeDtypeStruct((B, N, C), F32),
        ),
        in_specs=[smem, smem] + [vmem] * 7 + [hbm] * 4,
        out_specs=(hbm, hbm),
        scratch_shapes=[
            V((B, N, C), BF16),
            V((B, K_E, N, N), BF16),
            V((B, N, C), BF16),
            V((B, K_T, N, N), BF16),
            V((C, C), F32),
            V((ALL, N, C), F32),
            V((ALL, N, C), F32),
            V((ALL, N, C), F32),
            V((ALL, N, C), F32),
            V((SWEEPS, ALL, N, C), BF16),
            V((B, N, K_E * N), BF16),
            V((SLOTS, N, SLOTS * N), BF16),
            V((B, N, K_T * N), BF16),
            V((SWEEPS, SLOTS, N, C), BF16),
            V((B, N, C), F32),
            V((B, N, C), F32),
            V((B, N, C), BF16),
            V((4, N, C), BF16),
            V((ALL, N, C), BF16),
            V((NZ, CAP, N, C), BF16),
            V((NZ, CAP, N, C), BF16),
            V((CAP + 1, N, C), F32),
            V((B, N, C), BF16),
            V((NZ, 8, C), jnp.int32),
            pltpu.SMEM((NZ, 8, C), jnp.int32),
            dma((7,)),
            dma((SWEEPS, LEVELS)),
            dma((SWEEPS, LEVELS)),
            dma((2,)),
            dma((2,)),
            dma((NZ,)),
            dma((NZ,)),
            dma((NZ,)),
            dma((NZ,)),
        ],
        compiler_params=pltpu.CompilerParams(
            collective_id=0, has_side_effects=True, vmem_limit_bytes=48 * 1024 * 1024
        ),
    )(
        tab,
        reference_material_kappas,
        ends,
        voltage_self_admittance,
        interface_admittance,
        warmth_self_coefficient,
        substance_kind,
        warmth_storage_per_point,
        layer_boundary_couplings,
        injected_amperage,
        voltage_coupling_tiles,
        warmth_values,
        warmth_coupling_tiles,
    )


def solution(mesh):
    both = ("elec", "therm")

    def split(rank):
        return P(both, *([None] * (rank - 1)))

    return jax.shard_map(
        body,
        mesh=mesh,
        in_specs=(
            split(3),
            split(2),
            split(4),
            split(2),
            split(2),
            split(3),
            split(2),
            split(1),
            split(3),
            split(2),
            split(4),
            split(2),
            split(3),
            split(2),
            P(),
            split(2),
        ),
        out_specs=(split(3), split(3)),
        check_vma=False,
    )
```

time: 202 us -> 95.2 us (0.47)
  Pallas kernels: 0 us -> 76 us
  starting transfers between devices: 73.1 us -> 0 us
  matrix products: 33 us -> 0 us
  waiting for transfers between devices: 20.4 us -> 0 us
  blocking collectives: 19.4 us -> 0 us
  local copies, waits for them, and re-layouts: 30 us -> 12.5 us
  between operations: 15.3 us -> 0.68 us
  other arithmetic: 9.18 us -> 4.72 us
    pallas_call x0 -> x1, Pallas kernels: none -> 76 us  [body(): pl.pallas_call(kernel, out_shape=(jax.ShapeDtypeStruct((B, N, C), BF16),...]
    ppermute x22 -> x0, starting transfers between devices: 73 us -> none  [the longest x20 67.5 us: from_partner(): return lax.ppermute(block, axis, route)]
    dot_general x19 -> x0, matrix products: 33 us -> none  [the longest x6 23.4 us: near_product(): jnp.einsum('rkab,rkbc->rac', near_blocks, picked, preferred_element_type=...]
    gather x26 -> x0, local copies, waits for them, and re-layouts: 24 us -> none  [the longest x6 12.8 us: near_product(): picked = field_b[near_index]]
    all_gather x1 -> x0, waiting for transfers between devices: 20.3 us -> none  [body(): heat_piece = lax.all_gather(heat_b, 'therm', axis=0, tiled=True)]
    unnamed x1 -> x0, blocking collectives: 19.4 us -> none
    unnamed x35 -> x24, local copies, waits for them, and re-layouts: 4.18 us -> 12.1 us
    scatter-add x2 -> x0, other arithmetic: 3.31 us -> none  [body(): warmth_spread_operator.at[:ZB].add(low_terms).at[warmth_tile_count - ZB:]]
  transfers between devices with their start and end apart: 23 -> 0, of which waited for: 1 -> 0; matrix products, arithmetic and copies ran while one was open for 14% -> 0% of each run, Pallas kernels for 0% -> 0%
where the time goes in v1:
time: 95.2 us; the launch traced here: 94 us
  Pallas kernels  76 us (80%)
  local copies, waits for them, and re-layouts  12.5 us (13%)
  other arithmetic  4.72 us (5%)
    pallas_call x1, Pallas kernels, body(): pl.pallas_call(kernel, out_shape=(jax.ShapeDtypeStruct((B, N, C), BF16),...  76 us
    unnamed x24, local copies, waits for them, and re-layouts  12.1 us

profile of v1, /device:TPU:6, one launch (start us, length us, event | category | flops | bytes accessed | tf_op | source)
XLA Modules:
  0.0 94.0 jit_solution(6242839180840932890)
XLA Ops:
  0.6 0.9 convert_reduce_fusion.1
  1.6 0.7 iota_compare_fusion.3
  2.2 0.8 copy.26
  3.2 0.7 compare_select_fusion.1
  3.9 0.8 select_reduce_fusion.1
  4.7 0.7 compare_select_fusion
  5.4 0.7 iota_compare_fusion
  6.1 0.1 convert_reduce_fusion
  6.3 0.1 reshape.82
  6.4 0.8 copy.28
  7.2 0.1 reshape.83
  7.4 1.4 %copy-done = bf16[32,3,64,64]{3,2,1,0:T(8,128)(2,1)S(1)} copy-done((bf16[32,3,64,64]{3,2,1,0:T(8,128)(2,1)S(1)}, bf16[32,3,64,64]{3,2,1,0:T(8,128)(2,1)}, u32[]{:S(2)}) %copy-start) | copy-done | bytes 786456
  8.8 1.0 %copy-done.1 = bf16[32,64,128]{2,1,0:T(8,128)(2,1)S(1)} copy-done((bf16[32,64,128]{2,1,0:T(8,128)(2,1)S(1)}, bf16[32,64,128]{2,1,0:T(8,128)(2,1)}, u32[]{:S(2)}) %copy-start.1) | copy-done | bytes 524312
  9.8 1.0 %copy-done.2 = bf16[32,64,128]{2,1,0:T(8,128)(2,1)S(1)} copy-done((bf16[32,64,128]{2,1,0:T(8,128)(2,1)S(1)}, bf16[32,64,128]{2,1,0:T(8,128)(2,1)}, u32[]{:S(2)}) %copy-start.2) | copy-done | bytes 524312
  10.9 0.9 copy-done.3
  11.8 0.8 copy-done.4
  12.6 0.7 copy-done.5
  13.3 0.7 copy-done.6
  14.1 0.7 copy-done.7
  14.8 0.7 copy-done.8
  15.5 0.7 copy-done.9
  16.1 76.0 %shard_map.167 = (bf16[32,64,128]{2,1,0:T(8,128)(2,1)S(1)}, f32[32,64,128]{2,1,0:T(8,128)S(1)}) custom-call(s32[360]{0:T(512)S(1)} %concatenate.3.tab, f32[8]{0:T(128)S(1)} %copy-done.9, s32[8,8,128]{2,1,0:T(8,128)S(1)} %broadcast_in_dim.54.ends, f32[32,64]{1,0:T(8,128)S(1)} %copy-done.5, bf16[8,64,64]{2,1,0:T(8,128)(2,1)S(1)} %copy-done.3, ...), custom_call_target="tpu_custom_call" | custom-call | tf_op jit(solution)/shard_map/pallas_call | solution.py:422
  92.2 0.8 copy.31
  93.0 1.0 %copy.32 = f32[32,64,128]{2,1,0:T(8,128)} copy(f32[32,64,128]{2,1,0:T(8,128)S(1)} %get-tuple-element.7) | data formatting | bytes 2097152
  (18 shorter events, 0.5 us)
Async XLA Ops:
  7.4 1.4 %copy-start = (bf16[32,3,64,64]{3,2,1,0:T(8,128)(2,1)S(1)}, bf16[32,3,64,64]{3,2,1,0:T(8,128)(2,1)}, u32[]{:S(2)}) copy-start(bf16[32,3,64,64]{3,2,1,0:T(8,128)(2,1)} %ttiles_h.1) | copy-start | bytes 2359300
  8.8 1.0 %copy-start.1 = (bf16[32,64,128]{2,1,0:T(8,128)(2,1)S(1)}, bf16[32,64,128]{2,1,0:T(8,128)(2,1)}, u32[]{:S(2)}) copy-start(bf16[32,64,128]{2,1,0:T(8,128)(2,1)} %source_h.1) | copy-start | bytes 1572868
  9.8 1.0 %copy-start.2 = (bf16[32,64,128]{2,1,0:T(8,128)(2,1)S(1)}, bf16[32,64,128]{2,1,0:T(8,128)(2,1)}, u32[]{:S(2)}) copy-start(bf16[32,64,128]{2,1,0:T(8,128)(2,1)} %warm_h.1) | copy-start | bytes 1572868
  10.9 0.9 copy-start.3
  11.8 0.8 copy-start.4
  12.6 0.7 copy-start.5
  13.3 0.7 copy-start.6
  14.1 0.7 copy-start.7
  14.8 0.7 copy-start.8
  15.5 0.7 copy-start.9

commit v2 on v1

--- a/solution.py
+++ b/solution.py
@@ -25,12 +25,11 @@
 K_T = 3
 ALL = B + SLOTS
 
-AT_IDS = 0
-AT_SRC = AT_IDS + B * K_E
-AT_OUT = AT_SRC + ALL
-AT_PACK = AT_OUT + B
-AT_TIDS = AT_PACK + NZ * CAP
-AT_END = AT_TIDS + B * K_T
+ROW_IDS = 0
+ROW_TIDS = ROW_IDS + K_E
+ROW_OUT = ROW_TIDS + K_T
+ROW_PACK = ROW_OUT + 1
+ROWS = 16
 
 
 def loop(n, step, unroll=1, start=0):
@@ -42,26 +41,45 @@
 
 
 def kernel(
-    tab,
+    kappas_h,
+    conn_h,
+    sends_h,
+    owner_h,
+    row_h,
+    tconn_h,
+    diag_e_h,
+    faces_h,
+    diag_t_h,
+    kind_h,
+    storage_h,
+    rims_h,
+    source_h,
+    tiles_h,
+    warm_h,
+    ttiles_h,
+    v_out,
+    acc,
     kappas,
-    ends,
+    sends,
+    conn,
+    owner,
+    row,
+    tconn,
     diag_e,
     faces,
     diag_t,
     kind,
     storage,
     rims,
-    source_h,
-    tiles_h,
-    warm_h,
-    ttiles_h,
-    v_out,
-    w_out,
     source,
     tiles,
     warm,
     ttiles,
+    tab_v,
+    tab,
+    ends,
     turn,
+    iturn,
     scale,
     diag,
     start0,
@@ -72,14 +90,12 @@
     tnear,
     inc,
     coef,
-    acc,
     flux,
     halo,
     heat,
     outgo,
     income,
     prefix,
-    vbuf,
     ends_in,
     ends_s,
     local_sem,
@@ -98,11 +114,26 @@
     def copy_in(src, dst, i):
         return pltpu.make_async_copy(src, dst, local_sem.at[i])
 
-    c_source = copy_in(source_h, source, 0)
-    c_tiles = copy_in(tiles_h, tiles, 1)
-    c_warm = copy_in(warm_h, warm, 2)
-    c_ttiles = copy_in(ttiles_h, ttiles, 3)
-    for c in (c_source, c_tiles, c_warm, c_ttiles):
+    pairs = (
+        (diag_e_h, diag_e),
+        (source_h, source),
+        (sends_h, sends),
+        (conn_h, conn),
+        (tconn_h, tconn),
+        (owner_h, owner),
+        (row_h, row),
+        (faces_h, faces),
+        (tiles_h, tiles),
+        (warm_h, warm),
+        (kappas_h, kappas),
+        (kind_h, kind),
+        (diag_t_h, diag_t),
+        (storage_h, storage),
+        (rims_h, rims),
+        (ttiles_h, ttiles),
+    )
+    loads = [copy_in(src, dst, i) for i, (src, dst) in enumerate(pairs)]
+    for c in loads:
         c.start()
 
     def partner(bit):
@@ -137,9 +168,11 @@
         )
 
     turn[...] = jnp.zeros_like(turn)
+    loads[0].wait()
     turn[0:B, 0:N] = RELAX / diag_e[...]
     turn[B : 2 * B, 0:N] = diag_e[...]
-    c_source.wait()
+    loads[1].wait()
+    loads[2].wait()
     flipped = turn[...].T[0:N, :]
 
     def first(i, cur):
@@ -155,58 +188,93 @@
 
     lax.fori_loop(0, B, first, flipped, unroll=2)
 
-    def slot_copy(m):
-        i = tab[AT_SRC + m]
-        field[0, m] = field[0, i]
-
-    loop(ALL, slot_copy, 8, B)
+    tiles_of_slots = [sends[s % 2, s // 2] for s in range(SLOTS)]
+    for s in range(SLOTS):
+        field[0, B + s] = field[0, tiles_of_slots[s]]
     pl.semaphore_wait(barrier, LEVELS + NZ - 1)
     for b in reversed(range(LEVELS)):
         exchange(0, b).start()
 
-    c_ends = [give(ends.at[lax.rem(t + o, NZ)], ends_in.at[o], ends_send.at[o], ends_recv.at[o], o) for o in range(1, NZ)]
+    def moved(x):
+        hit = x
+        for s in reversed(range(SLOTS)):
+            hit = jnp.where(x == tiles_of_slots[s], B + s, hit)
+        return hit
+
+    for i in range(3, 7):
+        loads[i].wait()
+    tab_v[...] = jnp.zeros_like(tab_v)
+    tab_v[ROW_IDS : ROW_IDS + K_E, 0:B] = moved(conn[...])
+    tab_v[ROW_TIDS : ROW_TIDS + K_T, 0:B] = tconn[...]
+    tab_v[ROW_OUT : ROW_OUT + 1, 0:B] = moved(lax.broadcasted_iota(jnp.int32, (1, B), 1))
+    iturn[...] = jnp.zeros_like(iturn)
+    iturn[0:1, 0:B] = owner[...]
+    iturn[1:2, 0:B] = row[...]
+    columns = iturn[...].T
+    block = lax.broadcasted_iota(jnp.int32, (B, C), 0)
+    lane = lax.broadcasted_iota(jnp.int32, (B, C), 1)
+    own_c = jnp.broadcast_to(columns[0:B, 0:1], (B, C))
+    row_c = jnp.broadcast_to(columns[0:B, 1:2], (B, C))
+    own_r = jnp.broadcast_to(iturn[0:1, :], (B, C))
+    row_r = jnp.broadcast_to(iturn[1:2, :], (B, C))
+    earlier = (own_r == own_c) & (lane < B) & (row_r * B + lane < row_c * B + block)
+    rank = jnp.sum(jnp.where(earlier, 1.0, 0.0), axis=1, keepdims=True).astype(jnp.int32)
+    place_c = own_c * CAP + jnp.broadcast_to(rank, (B, C))
+    packed = jnp.where(place_c == lane, moved(block), 0)
+    tab_v[ROW_PACK : ROW_PACK + 1, :] = jnp.clip(
+        jnp.sum(packed, axis=0, keepdims=True), 0, ALL - 1
+    )
+    c_tab = copy_in(tab_v, tab, 16)
+    c_tab.start()
+
+    for z in range(NZ):
+        before = jnp.where((own_c == z) & (row_c < lane), 1, 0)
+        ends[z, 0:1, :] = jnp.clip(jnp.sum(before, axis=0, keepdims=True), 0, CAP)
+        ends[z, 1:8, :] = jnp.zeros((7, C), jnp.int32)
+    c_ends = [
+        give(ends.at[lax.rem(t + o, NZ)], ends_in.at[o], ends_send.at[o], ends_recv.at[o], o)
+        for o in range(1, NZ)
+    ]
     for c in c_ends:
         c.start()
     ends_in[0] = ends[t]
 
-    def slot_more(m):
-        i = tab[AT_SRC + m]
-        scale[m] = scale[i]
-        diag[m] = diag[i]
-        start0[m] = start0[i]
-        pot[m] = start0[i]
-
-    loop(ALL, slot_more, 2, B)
-
+    for s in range(SLOTS):
+        i = tiles_of_slots[s]
+        scale[B + s] = scale[i]
+        diag[B + s] = diag[i]
+        start0[B + s] = start0[i]
+        pot[B + s] = start0[i]
+
+    loads[7].wait()
     for s in range(SLOTS):
         for q in range(SLOTS):
-            same = (tab[AT_SRC + B + s] == tab[AT_SRC + B + q]).astype(F32)
+            same = (tiles_of_slots[s] == tiles_of_slots[q]).astype(F32)
             wide[s, :, q * N : (q + 1) * N] = (faces[q].astype(F32) * same).astype(BF16)
 
-    c_tiles.wait()
+    loads[8].wait()
 
     def lay_e(i):
         near[i] = jnp.concatenate([tiles[i, k] for k in range(K_E)], axis=1)
 
     loop(B, lay_e, 2)
-
-    def product(k, m):
-        i = tab[AT_SRC + m]
-        rhs = jnp.concatenate(
-            [field[k, tab[AT_IDS + i * K_E + q]] for q in range(K_E)], axis=0
-        )
+    c_tab.wait()
+
+    def product(k, i):
+        rhs = jnp.concatenate([field[k, tab[ROW_IDS + q, i]] for q in range(K_E)], axis=0)
         return jnp.dot(near[i], rhs, preferred_element_type=F32)
 
     def sweep(k):
-        def update(m):
-            new = pot[m] + start0[m] - RELAX * field[k, m].astype(F32) - scale[m] * product(k, m)
+        def update(m, i):
+            new = pot[m] + start0[m] - RELAX * field[k, m].astype(F32) - scale[m] * product(k, i)
             pot[m] = new
             return new
 
-        loop(ALL, update, 4, B)
+        for s in range(SLOTS):
+            update(B + s, tiles_of_slots[s])
 
         def natural(m):
-            field[k + 1, m] = update(m).astype(BF16)
+            field[k + 1, m] = update(m, m).astype(BF16)
 
         loop(B, natural, 4)
 
@@ -236,7 +304,8 @@
     c_up = give(flux.at[pl.ds(B - 2, 2)], halo.at[pl.ds(0, 2)], halo_send.at[0], halo_recv.at[0], 1)
     c_down = give(flux.at[pl.ds(0, 2)], halo.at[pl.ds(2, 2)], halo_send.at[1], halo_recv.at[1], NZ - 1)
     sweep(1)
-    c_warm.wait()
+    for i in range(9, 15):
+        loads[i].wait()
     kap = jnp.zeros((B, N), F32)
     for m in range(8):
         kap = kap + jnp.where(kind[...] == m, kappas[m], 0.0)
@@ -261,7 +330,7 @@
     c_down.start()
     finish(1)
     sweep(2)
-    c_ttiles.wait()
+    loads[15].wait()
 
     def lay_t(i):
         tnear[i] = jnp.concatenate([ttiles[i, k] for k in range(K_T)], axis=1)
@@ -271,7 +340,7 @@
     sweep(3)
 
     def conduct(i):
-        rhs = jnp.concatenate([flux[tab[AT_TIDS + i * K_T + q]] for q in range(K_T)], axis=0)
+        rhs = jnp.concatenate([flux[tab[ROW_TIDS + q, i]] for q in range(K_T)], axis=0)
         acc[i] = acc[i] - coef[i] * jnp.dot(tnear[i], rhs, preferred_element_type=F32)
 
     loop(B, conduct, 4)
@@ -279,10 +348,8 @@
 
     last = SWEEPS - 1
 
-    def slot_current(m):
-        pot[m] = diag[m] * field[last, m].astype(F32) + product(last, m)
-
-    loop(ALL, slot_current, 4, B)
+    for s in range(SLOTS):
+        pot[B + s] = diag[B + s] * field[last, B + s].astype(F32) + product(last, tiles_of_slots[s])
 
     def natural_heat(m):
         f = field[last, m].astype(F32)
@@ -291,11 +358,9 @@
     loop(B, natural_heat, 4)
 
     def place(i):
-        vbuf[i] = field[last, tab[AT_OUT + i]]
+        v_out[i] = field[last, tab[ROW_OUT, i]]
 
     loop(B, place, 4)
-    c_v = copy_in(vbuf, v_out, 4)
-    c_v.start()
 
     c_up.wait()
     c_down.wait()
@@ -306,7 +371,7 @@
         acc[B - 2 + z] = acc[B - 2 + z] - jnp.where(t < NZ - 1, 1.0, 0.0) * coef[B - 2 + z] * high
     for c in c_ends:
         c.wait()
-    c_table = pltpu.make_async_copy(ends_in, ends_s, local_sem.at[5])
+    c_table = pltpu.make_async_copy(ends_in, ends_s, local_sem.at[17])
     c_table.start()
     c_table.wait()
 
@@ -322,10 +387,10 @@
     for o in order:
         to = lax.rem(t + o, NZ)
         for s in range(CAP):
-            outgo[o, s] = heat[tab[AT_PACK + to * CAP + s]]
+            outgo[o, s] = heat[tab[ROW_PACK, to * CAP + s]]
         c_heat[o].start()
     for s in range(CAP):
-        income[0, s] = heat[tab[AT_PACK + t * CAP + s]]
+        income[0, s] = heat[tab[ROW_PACK, t * CAP + s]]
 
     def collect(o):
         run = jnp.zeros((N, C), F32)
@@ -345,48 +410,11 @@
     for o in order:
         c_heat[o].wait_recv()
         collect(o)
-    c_w = copy_in(acc, w_out, 6)
-    c_w.start()
     for o in order:
         c_heat[o].wait_send()
     for k in range(SWEEPS):
         for b in range(LEVELS):
             exchange(k, b).wait_send()
-    c_v.wait()
-    c_w.wait()
-
-
-def tables(conn, sends, owner, row, tconn):
-    targets = sends.reshape(-1)
-    far = jnp.int32(1000)
-    slot = jnp.arange(SLOTS, dtype=jnp.int32)
-    block = jnp.arange(B, dtype=jnp.int32)
-
-    def moved(x):
-        hit = jnp.min(jnp.where(x[..., None] == targets, B + slot, far), axis=-1)
-        return jnp.where(hit < far, hit, x)
-
-    own = owner[:, 0]
-    earlier = (row[None, :] < row[:, None]) | (
-        (row[None, :] == row[:, None]) & (block[None, :] < block[:, None])
-    )
-    rank = jnp.sum(((own[None, :] == own[:, None]) & earlier).astype(jnp.int32), axis=1)
-    places = own * CAP + rank
-    spots = jnp.arange(NZ * CAP, dtype=jnp.int32)
-    at = moved(block)
-    pack = jnp.sum(jnp.where(places[None, :] == spots[:, None], at[None, :], 0), axis=1)
-    tab = jnp.concatenate(
-        [moved(conn).reshape(-1), block, targets, at, pack, tconn.reshape(-1)]
-    )
-    upto = jnp.arange(C, dtype=jnp.int32)
-    z = jnp.arange(NZ, dtype=jnp.int32)
-    ends = jnp.sum(
-        (
-            (own[None, None, :] == z[:, None, None]) & (row[None, None, :] < upto[None, :, None])
-        ).astype(jnp.int32),
-        axis=2,
-    )
-    return tab, jnp.broadcast_to(ends[:, None, :], (NZ, 8, C))
 
 
 def body(
@@ -407,32 +435,41 @@
     reference_material_kappas,
     warmth_storage_per_point,
 ):
-    tab, ends = tables(
-        voltage_partner_tile_ids,
-        interface_tiles_per_level,
-        warmth_receiver_layer,
-        warmth_receiver_tile,
-        warmth_partner_tile_ids,
-    )
-    smem = pl.BlockSpec(memory_space=pltpu.SMEM)
     vmem = pl.BlockSpec(memory_space=pltpu.VMEM)
-    hbm = pl.BlockSpec(memory_space=pl.ANY)
+    hbm = pl.BlockSpec(memory_space=pltpu.HBM)
     dma = pltpu.SemaphoreType.DMA
     V = pltpu.VMEM
+    I32 = jnp.int32
     return pl.pallas_call(
         kernel,
         out_shape=(
             jax.ShapeDtypeStruct((B, N, C), BF16),
             jax.ShapeDtypeStruct((B, N, C), F32),
         ),
-        in_specs=[smem, smem] + [vmem] * 7 + [hbm] * 4,
-        out_specs=(hbm, hbm),
+        in_specs=[hbm] * 16,
+        out_specs=(vmem, vmem),
         scratch_shapes=[
+            pltpu.SMEM((8,), F32),
+            pltpu.SMEM((2, LEVELS), I32),
+            V((K_E, B), I32),
+            V((1, B), I32),
+            V((1, B), I32),
+            V((K_T, B), I32),
+            V((B, N), F32),
+            V((SLOTS, N, N), BF16),
+            V((B, N), F32),
+            V((B, N), I32),
+            V((B, N), F32),
+            V((4, N, N), BF16),
             V((B, N, C), BF16),
             V((B, K_E, N, N), BF16),
             V((B, N, C), BF16),
             V((B, K_T, N, N), BF16),
+            V((ROWS, C), I32),
+            pltpu.SMEM((ROWS, C), I32),
+            V((NZ, 8, C), I32),
             V((C, C), F32),
+            V((C, C), I32),
             V((ALL, N, C), F32),
             V((ALL, N, C), F32),
             V((ALL, N, C), F32),
@@ -443,17 +480,15 @@
             V((B, N, K_T * N), BF16),
             V((SWEEPS, SLOTS, N, C), BF16),
             V((B, N, C), F32),
-            V((B, N, C), F32),
             V((B, N, C), BF16),
             V((4, N, C), BF16),
             V((ALL, N, C), BF16),
             V((NZ, CAP, N, C), BF16),
             V((NZ, CAP, N, C), BF16),
             V((CAP + 1, N, C), F32),
-            V((B, N, C), BF16),
-            V((NZ, 8, C), jnp.int32),
-            pltpu.SMEM((NZ, 8, C), jnp.int32),
-            dma((7,)),
+            V((NZ, 8, C), I32),
+            pltpu.SMEM((NZ, 8, C), I32),
+            dma((18,)),
             dma((SWEEPS, LEVELS)),
             dma((SWEEPS, LEVELS)),
             dma((2,)),
@@ -464,12 +499,15 @@
             dma((NZ,)),
         ],
         compiler_params=pltpu.CompilerParams(
-            collective_id=0, has_side_effects=True, vmem_limit_bytes=48 * 1024 * 1024
+            collective_id=0, has_side_effects=True, vmem_limit_bytes=63 * 1024 * 1024
         ),
     )(
-        tab,
         reference_material_kappas,
-        ends,
+        voltage_partner_tile_ids.T,
+        interface_tiles_per_level.T,
+        warmth_receiver_layer.T,
+        warmth_receiver_tile.reshape(1, B),
+        warmth_partner_tile_ids.T,
         voltage_self_admittance,
         interface_admittance,
         warmth_self_coefficient,

time: 95.2 us -> 82.9 us (0.87)
  local copies, waits for them, and re-layouts: 12.5 us -> 4.17 us
  other arithmetic: 4.72 us -> 0 us
  Pallas kernels: 76 us -> 77.3 us
    unnamed x24 -> x2, local copies, waits for them, and re-layouts: 12.1 us -> 4.17 us
    select_n x2 -> x0, other arithmetic: 1.35 us -> none  [moved(): return jnp.where(hit < far, hit, x)]
    pallas_call x1, Pallas kernels: 76 us -> 77.3 us  [body(): pl.pallas_call(kernel, out_shape=(jax.ShapeDtypeStruct((B, N, C), BF16),...]
    reduce_sum x3 -> x0, other arithmetic: 1.12 us -> none  [the longest x1 0.91 us: tables(): jnp.sum(((own[None, :] == own[:, None]) & earlier).astype(jnp.int32), axi...]
where the time goes in v2:
time: 82.9 us; the launch traced here: 82.1 us
  Pallas kernels  77.3 us (93%)
  local copies, waits for them, and re-layouts  4.17 us (5%)
    pallas_call x1, Pallas kernels, body(): pl.pallas_call(kernel, out_shape=(jax.ShapeDtypeStruct((B, N, C), BF16),...  77.3 us
    unnamed x2, local copies, waits for them, and re-layouts  4.17 us

profile of v2, /device:TPU:6, one launch (start us, length us, event | category | flops | bytes accessed | tf_op | source)
XLA Modules:
  0.0 82.1 jit_solution(10518072354263880854)
XLA Ops:
  0.6 77.3 %shard_map.167 = (bf16[32,64,128]{2,1,0:T(8,128)(2,1)}, f32[32,64,128]{2,1,0:T(8,128)}) custom-call(f32[8]{0:T(128)} %kappas_h.1, s32[4,32]{1,0:T(4,128)} %bitcast.5, s32[2,4]{1,0:T(2,128)} %bitcast.7, s32[1,32]{1,0:T(1,128)} %bitcast.8, s32[1,32]{1,0:T(1,128)} %bitcast.9, s32[3,32]{1,0:T(4,128)} %bitcast.6, f32[32,64]{1,0:T(8,128)} %diag_e_h.1, ...), custom_call_target="tpu_custom_call" | custom-call | tf_op jit(solution)/shard_map/pallas_call | solution.py:443
  78.0 1.9 %copy.20 = bf16[32,64,128]{2,1,0:T(8,128)(2,1)} copy(bf16[32,64,128]{2,1,0:T(8,128)(2,1)} %get-tuple-element.4) | data formatting | bytes 1048576
  79.8 2.3 %copy.21 = f32[32,64,128]{2,1,0:T(8,128)} copy(f32[32,64,128]{2,1,0:T(8,128)} %get-tuple-element.5) | data formatting | bytes 2097152

commit v3 on v2

--- a/solution.py
+++ b/solution.py
@@ -30,14 +30,19 @@
 ROW_OUT = ROW_TIDS + K_T
 ROW_PACK = ROW_OUT + 1
 ROWS = 16
-
-
-def loop(n, step, unroll=1, start=0):
-    def one(i, _):
-        step(i)
+GROUP = 16
+PIECES = 4
+
+
+def grouped(n, size, read, write):
+    def one(g, _):
+        at = [g * size + u for u in range(size)]
+        got = [read(m) for m in at]
+        for m, x in zip(at, got):
+            write(m, x)
         return 0
 
-    lax.fori_loop(start, n, one, 0, unroll=unroll)
+    lax.fori_loop(0, n // size, one, 0)
 
 
 def kernel(
@@ -57,8 +62,8 @@
     tiles_h,
     warm_h,
     ttiles_h,
-    v_out,
-    acc,
+    v_h,
+    w_h,
     kappas,
     sends,
     conn,
@@ -84,7 +89,12 @@
     diag,
     start0,
     pot,
-    field,
+    field0,
+    field1,
+    field2,
+    field3,
+    field4,
+    part,
     near,
     wide,
     tnear,
@@ -96,6 +106,8 @@
     outgo,
     income,
     prefix,
+    acc,
+    v_out,
     ends_in,
     ends_s,
     local_sem,
@@ -110,6 +122,8 @@
 ):
     e = lax.axis_index("elec")
     t = lax.axis_index("therm")
+    field = (field0, field1, field2, field3, field4)
+    last = SWEEPS - 1
 
     def copy_in(src, dst, i):
         return pltpu.make_async_copy(src, dst, local_sem.at[i])
@@ -149,7 +163,7 @@
 
     def exchange(k, b):
         return pltpu.make_async_remote_copy(
-            src_ref=field.at[k, pl.ds(B + 2 * b, 2)],
+            src_ref=field[k].at[pl.ds(B + 2 * b, 2)],
             dst_ref=inc.at[k, pl.ds(2 * b, 2)],
             send_sem=ex_send.at[k, b],
             recv_sem=ex_recv.at[k, b],
@@ -171,29 +185,47 @@
     loads[0].wait()
     turn[0:B, 0:N] = RELAX / diag_e[...]
     turn[B : 2 * B, 0:N] = diag_e[...]
+    flipped = turn[...].T[0:N, :]
     loads[1].wait()
     loads[2].wait()
-    flipped = turn[...].T[0:N, :]
-
-    def first(i, cur):
-        s = jnp.broadcast_to(cur[:, 0:1], (N, C))
-        d = jnp.broadcast_to(cur[:, B : B + 1], (N, C))
-        scale[i] = s
-        diag[i] = d
-        v = s * source[i].astype(F32)
-        start0[i] = v
-        pot[i] = v
-        field[0, i] = v.astype(BF16)
-        return pltpu.roll(cur, C - 1, 1)
-
-    lax.fori_loop(0, B, first, flipped, unroll=2)
-
     tiles_of_slots = [sends[s % 2, s // 2] for s in range(SLOTS)]
+    spot = lax.broadcasted_iota(jnp.int32, (N, C), 1)
+
+    def column(x, i):
+        return jnp.broadcast_to(
+            jnp.sum(jnp.where(spot == i, x, 0.0), axis=1, keepdims=True), (N, C)
+        )
+
     for s in range(SLOTS):
-        field[0, B + s] = field[0, tiles_of_slots[s]]
+        i = tiles_of_slots[s]
+        sc = column(flipped, i)
+        v = sc * source[i].astype(F32)
+        scale[B + s] = sc
+        start0[B + s] = v
+        pot[B + s] = v
+        field0[B + s] = v.astype(BF16)
     pl.semaphore_wait(barrier, LEVELS + NZ - 1)
     for b in reversed(range(LEVELS)):
         exchange(0, b).start()
+
+    def first(g, cur):
+        got = []
+        for u in range(8):
+            i = g * 8 + u
+            sc = jnp.broadcast_to(cur[:, u : u + 1], (N, C))
+            d = jnp.broadcast_to(cur[:, B + u : B + u + 1], (N, C))
+            got.append((i, sc, d, sc * source[i].astype(F32)))
+        for i, sc, d, v in got:
+            scale[i] = sc
+            diag[i] = d
+            start0[i] = v
+            pot[i] = v
+            field0[i] = v.astype(BF16)
+        return pltpu.roll(cur, C - 8, 1)
+
+    lax.fori_loop(0, B // 8, first, flipped)
+    for s in range(SLOTS):
+        diag[B + s] = column(flipped, tiles_of_slots[s] + B)
 
     def moved(x):
         hit = x
@@ -239,60 +271,60 @@
         c.start()
     ends_in[0] = ends[t]
 
-    for s in range(SLOTS):
-        i = tiles_of_slots[s]
-        scale[B + s] = scale[i]
-        diag[B + s] = diag[i]
-        start0[B + s] = start0[i]
-        pot[B + s] = start0[i]
-
     loads[7].wait()
     for s in range(SLOTS):
         for q in range(SLOTS):
             same = (tiles_of_slots[s] == tiles_of_slots[q]).astype(F32)
-            wide[s, :, q * N : (q + 1) * N] = (faces[q].astype(F32) * same).astype(BF16)
+            wide[s * N : (s + 1) * N, q * N : (q + 1) * N] = (faces[q].astype(F32) * same).astype(BF16)
 
     loads[8].wait()
 
-    def lay_e(i):
-        near[i] = jnp.concatenate([tiles[i, k] for k in range(K_E)], axis=1)
-
-    loop(B, lay_e, 2)
+    grouped(
+        B,
+        8,
+        lambda i: jnp.concatenate([tiles[i, k] for k in range(K_E)], axis=1),
+        lambda i, x: near.__setitem__(i, x),
+    )
     c_tab.wait()
 
     def product(k, i):
-        rhs = jnp.concatenate([field[k, tab[ROW_IDS + q, i]] for q in range(K_E)], axis=0)
+        rhs = jnp.concatenate([field[k][tab[ROW_IDS + q, i]] for q in range(K_E)], axis=0)
         return jnp.dot(near[i], rhs, preferred_element_type=F32)
 
     def sweep(k):
         def update(m, i):
-            new = pot[m] + start0[m] - RELAX * field[k, m].astype(F32) - scale[m] * product(k, i)
+            return pot[m] + start0[m] - RELAX * field[k][m].astype(F32) - scale[m] * product(k, i)
+
+        got = [update(B + s, tiles_of_slots[s]) for s in range(SLOTS)]
+        for s in range(SLOTS):
+            pot[B + s] = got[s]
+
+        def store(m, new):
             pot[m] = new
-            return new
-
+            field[k + 1][m] = new.astype(BF16)
+
+        grouped(B, GROUP, lambda m: update(m, m), store)
+
+    EARLY = (SLOTS - 2) * N
+
+    def face_terms(k, then):
+        for b in range(LEVELS - 1):
+            exchange(k, b).wait_recv()
+        part[...] = jnp.dot(
+            wide[:, 0:EARLY], inc[k, 0 : SLOTS - 2].reshape(EARLY, C), preferred_element_type=F32
+        )
+        exchange(k, LEVELS - 1).wait_recv()
+        total = part[...] + jnp.dot(
+            wide[:, EARLY:], inc[k, SLOTS - 2 :].reshape(2 * N, C), preferred_element_type=F32
+        )
         for s in range(SLOTS):
-            update(B + s, tiles_of_slots[s])
-
-        def natural(m):
-            field[k + 1, m] = update(m, m).astype(BF16)
-
-        loop(B, natural, 4)
-
-    def face_terms(k, then):
-        for b in range(LEVELS):
-            exchange(k, b).wait_recv()
-        rhs = inc[k].reshape(SLOTS * N, C)
-
-        def one(s):
-            then(s, jnp.dot(wide[s], rhs, preferred_element_type=F32))
-
-        loop(SLOTS, one, 4)
+            then(s, total[s * N : (s + 1) * N])
 
     def finish(k):
         def then(s, g):
             new = pot[B + s] - scale[B + s] * g
             pot[B + s] = new
-            field[k + 1, B + s] = new.astype(BF16)
+            field[k + 1][B + s] = new.astype(BF16)
 
         face_terms(k, then)
         for b in reversed(range(LEVELS)):
@@ -314,53 +346,60 @@
     turn[2 * B : 3 * B, 0:N] = STEP / storage[...]
     tflipped = turn[...].T[0:N, :]
 
-    def warmth(i, cur):
-        dt = jnp.broadcast_to(cur[:, 0:1], (N, C))
-        ka = jnp.broadcast_to(cur[:, B : B + 1], (N, C))
-        co = jnp.broadcast_to(cur[:, 2 * B : 2 * B + 1], (N, C))
-        w = warm[i].astype(F32)
-        fl = (ka * (1.0 + 0.4 * jnp.tanh(w)) * w).astype(BF16)
-        flux[i] = fl
-        coef[i] = co
-        acc[i] = w - co * (dt * fl.astype(F32))
-        return pltpu.roll(cur, C - 1, 1)
-
-    lax.fori_loop(0, B, warmth, tflipped, unroll=2)
+    def warmth(g, cur):
+        got = []
+        for u in range(8):
+            i = g * 8 + u
+            dt = jnp.broadcast_to(cur[:, u : u + 1], (N, C))
+            ka = jnp.broadcast_to(cur[:, B + u : B + u + 1], (N, C))
+            co = jnp.broadcast_to(cur[:, 2 * B + u : 2 * B + u + 1], (N, C))
+            w = warm[i].astype(F32)
+            fl = (ka * (1.0 + 0.4 * jnp.tanh(w)) * w).astype(BF16)
+            got.append((i, fl, co, w - co * (dt * fl.astype(F32))))
+        for i, fl, co, x in got:
+            flux[i] = fl
+            coef[i] = co
+            acc[i] = x
+        return pltpu.roll(cur, C - 8, 1)
+
+    lax.fori_loop(0, B // 8, warmth, tflipped)
     c_up.start()
     c_down.start()
     finish(1)
     sweep(2)
     loads[15].wait()
 
-    def lay_t(i):
-        tnear[i] = jnp.concatenate([ttiles[i, k] for k in range(K_T)], axis=1)
-
-    loop(B, lay_t, 2)
+    grouped(
+        B,
+        8,
+        lambda i: jnp.concatenate([ttiles[i, k] for k in range(K_T)], axis=1),
+        lambda i, x: tnear.__setitem__(i, x),
+    )
     finish(2)
     sweep(3)
 
     def conduct(i):
         rhs = jnp.concatenate([flux[tab[ROW_TIDS + q, i]] for q in range(K_T)], axis=0)
-        acc[i] = acc[i] - coef[i] * jnp.dot(tnear[i], rhs, preferred_element_type=F32)
-
-    loop(B, conduct, 4)
+        return acc[i] - coef[i] * jnp.dot(tnear[i], rhs, preferred_element_type=F32)
+
+    grouped(B, GROUP, conduct, lambda i, x: acc.__setitem__(i, x))
     finish(3)
 
-    last = SWEEPS - 1
-
+    got = [
+        diag[B + s] * field4[B + s].astype(F32) + product(last, tiles_of_slots[s])
+        for s in range(SLOTS)
+    ]
     for s in range(SLOTS):
-        pot[B + s] = diag[B + s] * field[last, B + s].astype(F32) + product(last, tiles_of_slots[s])
+        pot[B + s] = got[s]
 
     def natural_heat(m):
-        f = field[last, m].astype(F32)
-        heat[m] = (f * (diag[m] * f + product(last, m))).astype(BF16)
-
-    loop(B, natural_heat, 4)
-
-    def place(i):
-        v_out[i] = field[last, tab[ROW_OUT, i]]
-
-    loop(B, place, 4)
+        f = field4[m].astype(F32)
+        return (f * (diag[m] * f + product(last, m))).astype(BF16)
+
+    grouped(B, GROUP, natural_heat, lambda m, x: heat.__setitem__(m, x))
+    grouped(B, 8, lambda i: field4[tab[ROW_OUT, i]], lambda i, x: v_out.__setitem__(i, x))
+    c_v = copy_in(v_out, v_h, 18)
+    c_v.start()
 
     c_up.wait()
     c_down.wait()
@@ -376,7 +415,7 @@
     c_table.wait()
 
     def slot_heat(s, g):
-        heat[B + s] = (field[last, B + s].astype(F32) * (pot[B + s] + g)).astype(BF16)
+        heat[B + s] = (field4[B + s].astype(F32) * (pot[B + s] + g)).astype(BF16)
 
     face_terms(last, slot_heat)
 
@@ -402,19 +441,41 @@
         def row(j):
             upto = prefix[ends_s[o, 0, j + 1]]
             before = prefix[ends_s[o, 0, j]]
-            acc[j] = acc[j] + coef[j] * (upto - before)
-
-        loop(B, row, 2)
+            return acc[j] + coef[j] * (upto - before)
+
+        grouped(B, 4, row, lambda j, x: acc.__setitem__(j, x))
 
     collect(0)
     for o in order:
         c_heat[o].wait_recv()
         collect(o)
+    c_w = copy_in(acc, w_h, 19)
+    c_w.start()
     for o in order:
         c_heat[o].wait_send()
     for k in range(SWEEPS):
         for b in range(LEVELS):
             exchange(k, b).wait_send()
+    c_v.wait()
+    c_w.wait()
+
+
+def hand_over(v_h, w_h, v_out, w_out, v_mid, w_mid, sem_in, sem_out):
+    size = B // PIECES
+    ways = []
+    for i in range(PIECES):
+        piece = pl.ds(i * size, size)
+        ways.append((w_h.at[piece], w_mid.at[piece], w_out.at[piece], 0, i))
+        ways.append((v_h.at[piece], v_mid.at[piece], v_out.at[piece], 1, i))
+    ins = [pltpu.make_async_copy(a, b, sem_in.at[r, i]) for a, b, c, r, i in ways]
+    outs = [pltpu.make_async_copy(b, c, sem_out.at[r, i]) for a, b, c, r, i in ways]
+    for c in ins:
+        c.start()
+    for c, d in zip(ins, outs):
+        c.wait()
+        d.start()
+    for d in outs:
+        d.wait()
 
 
 def body(
@@ -435,19 +496,19 @@
     reference_material_kappas,
     warmth_storage_per_point,
 ):
-    vmem = pl.BlockSpec(memory_space=pltpu.VMEM)
     hbm = pl.BlockSpec(memory_space=pltpu.HBM)
     dma = pltpu.SemaphoreType.DMA
     V = pltpu.VMEM
     I32 = jnp.int32
-    return pl.pallas_call(
+    shapes = (
+        jax.ShapeDtypeStruct((B, N, C), BF16),
+        jax.ShapeDtypeStruct((B, N, C), F32),
+    )
+    v, w = pl.pallas_call(
         kernel,
-        out_shape=(
-            jax.ShapeDtypeStruct((B, N, C), BF16),
-            jax.ShapeDtypeStruct((B, N, C), F32),
-        ),
+        out_shape=shapes,
         in_specs=[hbm] * 16,
-        out_specs=(vmem, vmem),
+        out_specs=(hbm, hbm),
         scratch_shapes=[
             pltpu.SMEM((8,), F32),
             pltpu.SMEM((2, LEVELS), I32),
@@ -474,9 +535,14 @@
             V((ALL, N, C), F32),
             V((ALL, N, C), F32),
             V((ALL, N, C), F32),
-            V((SWEEPS, ALL, N, C), BF16),
+            V((ALL, N, C), BF16),
+            V((ALL, N, C), BF16),
+            V((ALL, N, C), BF16),
+            V((ALL, N, C), BF16),
+            V((ALL, N, C), BF16),
+            V((SLOTS * N, C), F32),
             V((B, N, K_E * N), BF16),
-            V((SLOTS, N, SLOTS * N), BF16),
+            V((SLOTS * N, SLOTS * N), BF16),
             V((B, N, K_T * N), BF16),
             V((SWEEPS, SLOTS, N, C), BF16),
             V((B, N, C), F32),
@@ -486,9 +552,11 @@
             V((NZ, CAP, N, C), BF16),
             V((NZ, CAP, N, C), BF16),
             V((CAP + 1, N, C), F32),
+            V((B, N, C), F32),
+            V((B, N, C), BF16),
             V((NZ, 8, C), I32),
             pltpu.SMEM((NZ, 8, C), I32),
-            dma((18,)),
+            dma((20,)),
             dma((SWEEPS, LEVELS)),
             dma((SWEEPS, LEVELS)),
             dma((2,)),
@@ -519,6 +587,14 @@
         warmth_values,
         warmth_coupling_tiles,
     )
+    return pl.pallas_call(
+        hand_over,
+        out_shape=shapes,
+        in_specs=[hbm, hbm],
+        out_specs=(hbm, hbm),
+        scratch_shapes=[V((B, N, C), BF16), V((B, N, C), F32), dma((2, PIECES)), dma((2, PIECES))],
+        compiler_params=pltpu.CompilerParams(vmem_limit_bytes=63 * 1024 * 1024),
+    )(v, w)
 
 
 def solution(mesh):

time: 82.9 us -> 67.2 us (0.81)
  Pallas kernels: 77.3 us -> 66.3 us
  local copies, waits for them, and re-layouts: 4.17 us -> 0 us
    pallas_call x1 -> x2, Pallas kernels: 77.3 us -> 66.3 us  [the longest x1 64.1 us: body(): pl.pallas_call(kernel, out_shape=shapes, in_specs=[hbm] * 16, out_specs=(...]
    unnamed x2 -> x0, local copies, waits for them, and re-layouts: 4.17 us -> none
where the time goes in v3:
time: 67.2 us; the launch traced here: 67 us
  Pallas kernels  66.3 us (99%)
    pallas_call x1, Pallas kernels, body(): pl.pallas_call(kernel, out_shape=shapes, in_specs=[hbm] * 16, out_specs=(...  64.1 us
    pallas_call x1, Pallas kernels, body(): pl.pallas_call(hand_over, out_shape=shapes, in_specs=[hbm, hbm], out_spec...  2.23 us

profile of v3, /device:TPU:6, one launch (start us, length us, event | category | flops | bytes accessed | tf_op | source)
XLA Modules:
  0.0 67.0 jit_solution(4714470675380289387)
XLA Ops:
  0.6 64.1 %shard_map.167 = (bf16[32,64,128]{2,1,0:T(8,128)(2,1)}, f32[32,64,128]{2,1,0:T(8,128)}) custom-call(f32[8]{0:T(128)} %kappas_h.1, s32[4,32]{1,0:T(4,128)} %bitcast.5, s32[2,4]{1,0:T(2,128)} %bitcast.7, s32[1,32]{1,0:T(1,128)} %bitcast.8, s32[1,32]{1,0:T(1,128)} %bitcast.9, s32[3,32]{1,0:T(4,128)} %bitcast.6, f32[32,64]{1,0:T(8,128)} %diag_e_h.1, ...), custom_call_target="tpu_custom_call" | custom-call | tf_op jit(solution)/shard_map/pallas_call | solution.py:507
  64.7 2.2 %shard_map.168 = (bf16[32,64,128]{2,1,0:T(8,128)(2,1)}, f32[32,64,128]{2,1,0:T(8,128)}) custom-call(bf16[32,64,128]{2,1,0:T(8,128)(2,1)} %get-tuple-element.4.v_h, f32[32,64,128]{2,1,0:T(8,128)} %get-tuple-element.5.w_h), custom_call_target="tpu_custom_call" | custom-call | tf_op jit(solution)/shard_map/pallas_call | solution.py:590

commit v4 on v3

--- a/solution.py
+++ b/solution.py
@@ -31,7 +31,6 @@
 ROW_PACK = ROW_OUT + 1
 ROWS = 16
 GROUP = 16
-PIECES = 4
 
 
 def grouped(n, size, read, write):
@@ -62,8 +61,8 @@
     tiles_h,
     warm_h,
     ttiles_h,
-    v_h,
-    w_h,
+    v_out,
+    acc,
     kappas,
     sends,
     conn,
@@ -106,8 +105,6 @@
     outgo,
     income,
     prefix,
-    acc,
-    v_out,
     ends_in,
     ends_s,
     local_sem,
@@ -398,8 +395,6 @@
 
     grouped(B, GROUP, natural_heat, lambda m, x: heat.__setitem__(m, x))
     grouped(B, 8, lambda i: field4[tab[ROW_OUT, i]], lambda i, x: v_out.__setitem__(i, x))
-    c_v = copy_in(v_out, v_h, 18)
-    c_v.start()
 
     c_up.wait()
     c_down.wait()
@@ -419,7 +414,7 @@
 
     face_terms(last, slot_heat)
 
-    order = (4, 3, 5, 2, 6, 1, 7)
+    order = (1, 7, 2, 6, 3, 5, 4)
     c_heat = {
         o: give(outgo.at[o], income.at[o], heat_send.at[o], heat_recv.at[o], o) for o in order
     }
@@ -449,33 +444,11 @@
     for o in order:
         c_heat[o].wait_recv()
         collect(o)
-    c_w = copy_in(acc, w_h, 19)
-    c_w.start()
     for o in order:
         c_heat[o].wait_send()
     for k in range(SWEEPS):
         for b in range(LEVELS):
             exchange(k, b).wait_send()
-    c_v.wait()
-    c_w.wait()
-
-
-def hand_over(v_h, w_h, v_out, w_out, v_mid, w_mid, sem_in, sem_out):
-    size = B // PIECES
-    ways = []
-    for i in range(PIECES):
-        piece = pl.ds(i * size, size)
-        ways.append((w_h.at[piece], w_mid.at[piece], w_out.at[piece], 0, i))
-        ways.append((v_h.at[piece], v_mid.at[piece], v_out.at[piece], 1, i))
-    ins = [pltpu.make_async_copy(a, b, sem_in.at[r, i]) for a, b, c, r, i in ways]
-    outs = [pltpu.make_async_copy(b, c, sem_out.at[r, i]) for a, b, c, r, i in ways]
-    for c in ins:
-        c.start()
-    for c, d in zip(ins, outs):
-        c.wait()
-        d.start()
-    for d in outs:
-        d.wait()
 
 
 def body(
@@ -496,19 +469,20 @@
     reference_material_kappas,
     warmth_storage_per_point,
 ):
+    vmem = pl.BlockSpec(memory_space=pltpu.VMEM)
     hbm = pl.BlockSpec(memory_space=pltpu.HBM)
     dma = pltpu.SemaphoreType.DMA
     V = pltpu.VMEM
     I32 = jnp.int32
     shapes = (
-        jax.ShapeDtypeStruct((B, N, C), BF16),
-        jax.ShapeDtypeStruct((B, N, C), F32),
-    )
-    v, w = pl.pallas_call(
+        V((B, N, C), BF16),
+        V((B, N, C), F32),
+    )
+    return pl.pallas_call(
         kernel,
         out_shape=shapes,
         in_specs=[hbm] * 16,
-        out_specs=(hbm, hbm),
+        out_specs=(vmem, vmem),
         scratch_shapes=[
             pltpu.SMEM((8,), F32),
             pltpu.SMEM((2, LEVELS), I32),
@@ -552,8 +526,6 @@
             V((NZ, CAP, N, C), BF16),
             V((NZ, CAP, N, C), BF16),
             V((CAP + 1, N, C), F32),
-            V((B, N, C), F32),
-            V((B, N, C), BF16),
             V((NZ, 8, C), I32),
             pltpu.SMEM((NZ, 8, C), I32),
             dma((20,)),
@@ -567,7 +539,7 @@
             dma((NZ,)),
         ],
         compiler_params=pltpu.CompilerParams(
-            collective_id=0, has_side_effects=True, vmem_limit_bytes=63 * 1024 * 1024
+            collective_id=0, has_side_effects=True, vmem_limit_bytes=61 * 1024 * 1024
         ),
     )(
         reference_material_kappas,
@@ -587,15 +559,6 @@
         warmth_values,
         warmth_coupling_tiles,
     )
-    return pl.pallas_call(
-        hand_over,
-        out_shape=shapes,
-        in_specs=[hbm, hbm],
-        out_specs=(hbm, hbm),
-        scratch_shapes=[V((B, N, C), BF16), V((B, N, C), F32), dma((2, PIECES)), dma((2, PIECES))],
-        compiler_params=pltpu.CompilerParams(vmem_limit_bytes=63 * 1024 * 1024),
-    )(v, w)
-
 
 def solution(mesh):
     both = ("elec", "therm")

time: 67.2 us -> 64.7 us (0.963)
  Pallas kernels: 66.3 us -> 62.1 us
  local copies, waits for them, and re-layouts: 0 us -> 1.77 us
    pallas_call x1 -> x0, Pallas kernels: 2.23 us -> none  [body(): pl.pallas_call(hand_over, out_shape=shapes, in_specs=[hbm, hbm], out_spec...]
    pallas_call x1, Pallas kernels: 64.1 us -> 62.1 us  [body(): pl.pallas_call(kernel, out_shape=shapes, in_specs=[hbm] * 16, out_specs=(...]
    unnamed x0 -> x2, local copies, waits for them, and re-layouts: none -> 1.77 us
where the time goes in v4:
time: 64.7 us; the launch traced here: 64.5 us
  Pallas kernels  62.1 us (96%)
  local copies, waits for them, and re-layouts  1.77 us (3%)
  between operations  0.65 us (1%)
    pallas_call x1, Pallas kernels, body(): pl.pallas_call(kernel, out_shape=shapes, in_specs=[hbm] * 16, out_specs=(...  62.1 us
    unnamed x2, local copies, waits for them, and re-layouts  1.77 us

profile of v4, /device:TPU:6, one launch (start us, length us, event | category | flops | bytes accessed | tf_op | source)
XLA Modules:
  0.0 64.5 jit_solution(12064636060413157583)
XLA Ops:
  0.6 62.1 %shard_map.167 = (bf16[32,64,128]{2,1,0:T(8,128)(2,1)S(1)}, f32[32,64,128]{2,1,0:T(8,128)S(1)}) custom-call(f32[8]{0:T(128)} %kappas_h.1, s32[4,32]{1,0:T(4,128)} %bitcast.5, s32[2,4]{1,0:T(2,128)} %bitcast.7, s32[1,32]{1,0:T(1,128)} %bitcast.8, s32[1,32]{1,0:T(1,128)} %bitcast.9, s32[3,32]{1,0:T(4,128)} %bitcast.6, f32[32,64]{1,0:T(8,128)} %diag_e_h.1, ...), custom_call_target="tpu_custom_call" | custom-call | tf_op jit(solution)/shard_map/pallas_call | solution.py:481
  62.7 0.8 %copy.20 = bf16[32,64,128]{2,1,0:T(8,128)(2,1)} copy(bf16[32,64,128]{2,1,0:T(8,128)(2,1)S(1)} %get-tuple-element.2) | data formatting | bytes 1048576
  63.5 1.0 %copy.21 = f32[32,64,128]{2,1,0:T(8,128)} copy(f32[32,64,128]{2,1,0:T(8,128)S(1)} %get-tuple-element.3) | data formatting | bytes 2097152

commit v5 on v4

--- a/solution.py
+++ b/solution.py
@@ -31,6 +31,8 @@
 ROW_PACK = ROW_OUT + 1
 ROWS = 16
 GROUP = 16
+FIRST = 7
+PIECES = 4
 
 
 def grouped(n, size, read, write):
@@ -144,14 +146,11 @@
         (ttiles_h, ttiles),
     )
     loads = [copy_in(src, dst, i) for i, (src, dst) in enumerate(pairs)]
-    for c in loads:
-        c.start()
-
     def partner(bit):
         return e + (1 << bit) - 2 * (1 << bit) * (lax.rem(lax.div(e, 1 << bit), 2))
 
     barrier = pltpu.get_barrier_semaphore()
-    for bit in range(LEVELS):
+    for bit in reversed(range(LEVELS)):
         pl.semaphore_signal(barrier, inc=1, device_id={"elec": partner(bit)}, device_id_type=MESH)
     for o in range(1, NZ):
         pl.semaphore_signal(
@@ -178,12 +177,17 @@
             device_id_type=MESH,
         )
 
+    for c in loads[:FIRST]:
+        c.start()
+
     turn[...] = jnp.zeros_like(turn)
     loads[0].wait()
     turn[0:B, 0:N] = RELAX / diag_e[...]
     turn[B : 2 * B, 0:N] = diag_e[...]
     flipped = turn[...].T[0:N, :]
     loads[1].wait()
+    for c in loads[FIRST:]:
+        c.start()
     loads[2].wait()
     tiles_of_slots = [sends[s % 2, s // 2] for s in range(SLOTS)]
     spot = lax.broadcasted_iota(jnp.int32, (N, C), 1)
@@ -304,28 +308,30 @@
 
     EARLY = (SLOTS - 2) * N
 
-    def face_terms(k, then):
+    def face_update(k, low, factor):
         for b in range(LEVELS - 1):
             exchange(k, b).wait_recv()
-        part[...] = jnp.dot(
+        some = jnp.dot(
             wide[:, 0:EARLY], inc[k, 0 : SLOTS - 2].reshape(EARLY, C), preferred_element_type=F32
         )
+        for s in range(SLOTS):
+            rows = slice(s * N, (s + 1) * N)
+            part[rows] = low(s) + factor(s) * some[rows]
         exchange(k, LEVELS - 1).wait_recv()
-        total = part[...] + jnp.dot(
+        more = jnp.dot(
             wide[:, EARLY:], inc[k, SLOTS - 2 :].reshape(2 * N, C), preferred_element_type=F32
         )
+        rows = [slice(s * N, (s + 1) * N) for s in range(SLOTS)]
+        return [part[rows[s]] + factor(s) * more[rows[s]] for s in range(SLOTS)]
+
+    def finish(k):
+        new = face_update(k, lambda s: pot[B + s], lambda s: -scale[B + s])
         for s in range(SLOTS):
-            then(s, total[s * N : (s + 1) * N])
-
-    def finish(k):
-        def then(s, g):
-            new = pot[B + s] - scale[B + s] * g
-            pot[B + s] = new
-            field[k + 1][B + s] = new.astype(BF16)
-
-        face_terms(k, then)
+            field[k + 1][B + s] = new[s].astype(BF16)
         for b in reversed(range(LEVELS)):
             exchange(k + 1, b).start()
+        for s in range(SLOTS):
+            pot[B + s] = new[s]
 
     sweep(0)
     finish(0)
@@ -409,10 +415,9 @@
     c_table.start()
     c_table.wait()
 
-    def slot_heat(s, g):
-        heat[B + s] = (field4[B + s].astype(F32) * (pot[B + s] + g)).astype(BF16)
-
-    face_terms(last, slot_heat)
+    current = face_update(last, lambda s: pot[B + s], lambda s: 1.0)
+    for s in range(SLOTS):
+        heat[B + s] = (field4[B + s].astype(F32) * current[s]).astype(BF16)
 
     order = (1, 7, 2, 6, 3, 5, 4)
     c_heat = {
@@ -449,6 +454,19 @@
     for k in range(SWEEPS):
         for b in range(LEVELS):
             exchange(k, b).wait_send()
+
+
+def hand_over(v, w, v_out, w_out, sems):
+    size = B // PIECES
+    copies = []
+    for i in range(PIECES):
+        piece = pl.ds(i * size, size)
+        copies.append(pltpu.make_async_copy(w.at[piece], w_out.at[piece], sems.at[0, i]))
+        copies.append(pltpu.make_async_copy(v.at[piece], v_out.at[piece], sems.at[1, i]))
+    for c in copies:
+        c.start()
+    for c in copies:
+        c.wait()
 
 
 def body(
@@ -478,7 +496,7 @@
         V((B, N, C), BF16),
         V((B, N, C), F32),
     )
-    return pl.pallas_call(
+    v, w = pl.pallas_call(
         kernel,
         out_shape=shapes,
         in_specs=[hbm] * 16,
@@ -559,6 +577,19 @@
         warmth_values,
         warmth_coupling_tiles,
     )
+    return pl.pallas_call(
+        hand_over,
+        out_shape=(
+            jax.ShapeDtypeStruct((B, N, C), BF16),
+            jax.ShapeDtypeStruct((B, N, C), F32),
+        ),
+        in_specs=[vmem, vmem],
+        out_specs=(hbm, hbm),
+        scratch_shapes=[dma((2, PIECES))],
+    )(
+        pltpu.with_memory_space_constraint(v, pltpu.VMEM),
+        pltpu.with_memory_space_constraint(w, pltpu.VMEM),
+    )
 
 def solution(mesh):
     both = ("elec", "therm")

time: 64.7 us -> 64.2 us (level)
  local copies, waits for them, and re-layouts: 1.77 us -> 0 us
  Pallas kernels: 62.1 us -> 63.4 us
    unnamed x2 -> x0, local copies, waits for them, and re-layouts: 1.77 us -> none
    pallas_call x0 -> x1, Pallas kernels: none -> 1.2 us  [body(): pl.pallas_call(hand_over, out_shape=(jax.ShapeDtypeStruct((B, N, C), BF16...]
where the time goes in v5:
time: 64.2 us; the launch traced here: 64 us
  Pallas kernels  63.4 us (99%)
    pallas_call x1, Pallas kernels, body(): pl.pallas_call(kernel, out_shape=shapes, in_specs=[hbm] * 16, out_specs=(...  62.2 us

profile of v5, /device:TPU:6, one launch (start us, length us, event | category | flops | bytes accessed | tf_op | source)
XLA Modules:
  0.0 64.0 jit_solution(2384225713712551187)
XLA Ops:
  0.6 62.2 %shard_map.167 = (bf16[32,64,128]{2,1,0:T(8,128)(2,1)S(1)}, f32[32,64,128]{2,1,0:T(8,128)S(1)}) custom-call(f32[8]{0:T(128)} %kappas_h.1, s32[4,32]{1,0:T(4,128)} %bitcast.5, s32[2,4]{1,0:T(2,128)} %bitcast.7, s32[1,32]{1,0:T(1,128)} %bitcast.8, s32[1,32]{1,0:T(1,128)} %bitcast.9, s32[3,32]{1,0:T(4,128)} %bitcast.6, f32[32,64]{1,0:T(8,128)} %diag_e_h.1, ...), custom_call_target="tpu_custom_call" | custom-call | tf_op jit(solution)/shard_map/pallas_call | solution.py:499
  62.8 1.2 %shard_map.168 = (bf16[32,64,128]{2,1,0:T(8,128)(2,1)}, f32[32,64,128]{2,1,0:T(8,128)}) custom-call(bf16[32,64,128]{2,1,0:T(8,128)(2,1)S(1)} %get-tuple-element.4.v, f32[32,64,128]{2,1,0:T(8,128)S(1)} %get-tuple-element.5.w), custom_call_target="tpu_custom_call" | custom-call | tf_op jit(solution)/shard_map/pallas_call | solution.py:580

commit v6 on v5

--- a/solution.py
+++ b/solution.py
@@ -30,8 +30,8 @@
 ROW_OUT = ROW_TIDS + K_T
 ROW_PACK = ROW_OUT + 1
 ROWS = 16
-GROUP = 16
-FIRST = 7
+GROUP = 8
+FIRST = 3
 PIECES = 4
 
 
@@ -419,15 +419,18 @@
     for s in range(SLOTS):
         heat[B + s] = (field4[B + s].astype(F32) * current[s]).astype(BF16)
 
-    order = (1, 7, 2, 6, 3, 5, 4)
-    c_heat = {
-        o: give(outgo.at[o], income.at[o], heat_send.at[o], heat_recv.at[o], o) for o in order
-    }
-    for o in order:
+    core = lax.rem(e, 2)
+    order = [
+        jnp.where(core == 0, x, y) for x, y in zip((1, 7, 2, 6, 3, 5, 4), (4, 3, 5, 2, 6, 1, 7))
+    ]
+    c_heat = [
+        give(outgo.at[o], income.at[o], heat_send.at[o], heat_recv.at[o], o) for o in order
+    ]
+    for o, c in zip(order, c_heat):
         to = lax.rem(t + o, NZ)
         for s in range(CAP):
             outgo[o, s] = heat[tab[ROW_PACK, to * CAP + s]]
-        c_heat[o].start()
+        c.start()
     for s in range(CAP):
         income[0, s] = heat[tab[ROW_PACK, t * CAP + s]]
 
@@ -446,11 +449,11 @@
         grouped(B, 4, row, lambda j, x: acc.__setitem__(j, x))
 
     collect(0)
-    for o in order:
-        c_heat[o].wait_recv()
+    for o, c in zip(order, c_heat):
+        c.wait_recv()
         collect(o)
-    for o in order:
-        c_heat[o].wait_send()
+    for c in c_heat:
+        c.wait_send()
     for k in range(SWEEPS):
         for b in range(LEVELS):
             exchange(k, b).wait_send()

time: 64.2 us -> 64.1 us (level)
  no operation moved by 1% of the time
where the time goes in v6:
time: 64.1 us; the launch traced here: 63.5 us
  Pallas kernels  62.8 us (98%)
    pallas_call x1, Pallas kernels, body(): pl.pallas_call(kernel, out_shape=shapes, in_specs=[hbm] * 16, out_specs=(...  61.6 us

profile of v6, /device:TPU:6, one launch (start us, length us, event | category | flops | bytes accessed | tf_op | source)
XLA Modules:
  0.0 63.5 jit_solution(1645425327117764039)
XLA Ops:
  0.6 61.6 %shard_map.167 = (bf16[32,64,128]{2,1,0:T(8,128)(2,1)S(1)}, f32[32,64,128]{2,1,0:T(8,128)S(1)}) custom-call(f32[8]{0:T(128)} %kappas_h.1, s32[4,32]{1,0:T(4,128)} %bitcast.5, s32[2,4]{1,0:T(2,128)} %bitcast.7, s32[1,32]{1,0:T(1,128)} %bitcast.8, s32[1,32]{1,0:T(1,128)} %bitcast.9, s32[3,32]{1,0:T(4,128)} %bitcast.6, f32[32,64]{1,0:T(8,128)} %diag_e_h.1, ...), custom_call_target="tpu_custom_call" | custom-call | tf_op jit(solution)/shard_map/pallas_call | solution.py:502
  62.3 1.2 %shard_map.168 = (bf16[32,64,128]{2,1,0:T(8,128)(2,1)}, f32[32,64,128]{2,1,0:T(8,128)}) custom-call(bf16[32,64,128]{2,1,0:T(8,128)(2,1)S(1)} %get-tuple-element.4.v, f32[32,64,128]{2,1,0:T(8,128)S(1)} %get-tuple-element.5.w), custom_call_target="tpu_custom_call" | custom-call | tf_op jit(solution)/shard_map/pallas_call | solution.py:583
